TPU v7x, 512 devices: a whole 4x4x16 slice. The times are simulated.
512 devices in a mesh: dp: 32 (over x, y, core), tensor: 16 (over z).
Axes of the slice: x: 4, y: 4, z: 16, core: 2. Of those that a mesh axis runs over, the one named last changes fastest.
Arguments:
- gate_pre: bfloat16 [4096, 26624], P('dp', 'tensor'), may hold values from -6 to 6
- up_pre: bfloat16 [4096, 26624], P('dp', 'tensor'), may hold values from -6 to 6
- grad_rot: bfloat16 [4096, 26624], P('dp', 'tensor'), may hold values from -6 to 6
- grad_out: bfloat16 [4096, 8192], P('dp', 'tensor'), may hold values from -0.119628906 to 0.119628906
- latent_weight: bfloat16 [26624, 8192], P('dp', 'tensor'), may hold values from -0.0390625 to 0.0390625
- clip_codes: int32 [8192], P('tensor'), may hold values from 20 to 139
- bits: int32 [8192], P('tensor'), may hold values from 3 to 8
Outputs:
- grad_gate: bfloat16 [4096, 26624], P('dp', 'tensor')
- grad_up: bfloat16 [4096, 26624], P('dp', 'tensor')
- grad_weight: bfloat16 [26624, 8192], P('dp', 'tensor')
All inputs are finite; a program needn't handle non-finite values.
Results may differ from a plain program's by a relative error of at most 0.014.
Values may be sent and summed in bfloat16 or wider, within the bound.
A program may use at most 64 MiB of HBM per device.

v0:
```python
import math

import jax
import jax.numpy as jnp
from jax import lax
from jax.sharding import PartitionSpec as P

HAD = 1024
NBLK = 26


def partner_2(value, axis, distance):
    mask = 2**distance
    pairs = [(source, source ^ mask) for source in range(lax.axis_size(axis))]
    return lax.ppermute(value, axis, pairs)


def sign_table(order):
    row_ids = jnp.arange(order, dtype=jnp.int32)[:, None]
    col_ids = jnp.arange(order, dtype=jnp.int32)[None, :]
    parity = jnp.zeros((order, order), jnp.int32)
    for position in range(order.bit_length() - 1):
        parity = parity + (jnp.right_shift(row_ids, position) & 1) * (
            jnp.right_shift(col_ids, position) & 1
        )
    signs = (1 - 2 * (parity % 2)).astype(jnp.float32)
    return (signs / jnp.sqrt(jnp.float32(order))).astype(jnp.bfloat16)


def apply_table(values, table_bf):
    rows_count = values.shape[0]
    order = table_bf.shape[0]
    shaped = values.reshape(rows_count, order, NBLK)
    turned = jnp.einsum("tpk,qp->tqk", shaped, table_bf, preferred_element_type=jnp.float32)
    return turned.reshape(rows_count, order * NBLK)


def local(gate_pre, up_pre, grad_rot, grad_out, latent_weight, clip_codes, bits):
    local_rows = gate_pre.shape[0]
    tensor_count = lax.axis_size("tensor")
    gate_vals = gate_pre.astype(jnp.float32)
    up_vals = up_pre.astype(jnp.float32)
    sigmoid_gate = jax.nn.sigmoid(gate_vals)
    hidden = (gate_vals * sigmoid_gate * up_vals).astype(jnp.bfloat16)
    full_table = sign_table(HAD)
    spread = lax.all_to_all(hidden, "tensor", split_axis=0, concat_axis=1, tiled=True)
    rotated = apply_table(spread, full_table).astype(jnp.bfloat16)
    blocks = lax.all_to_all(rotated, "dp", split_axis=1, concat_axis=0, tiled=True)
    feature_cols = grad_out.shape[1]
    grad_parts = grad_out.reshape(tensor_count, local_rows // tensor_count, feature_cols)
    grad_all = lax.all_gather(grad_parts, "dp", axis=1, tiled=True)
    grad_all = grad_all.reshape(grad_all.shape[0] * grad_all.shape[1], feature_cols)
    product = lax.dot_general(
        lax.all_gather(blocks, "tensor", axis=0, tiled=True),
        grad_all,
        (((0,), (0,)), ((), ())),
        preferred_element_type=jnp.float32,
    )
    levels = jnp.left_shift(jnp.int32(1), bits - 1) - 1
    clip_bound = clip_codes.astype(jnp.float32) * levels.astype(jnp.float32) / 65536.0
    inside = jnp.abs(latent_weight.astype(jnp.float32)) <= clip_bound[None, :]
    grad_weight = jnp.where(inside, product, 0.0).astype(jnp.bfloat16)
    local_table = sign_table(HAD // tensor_count)
    current = apply_table(grad_rot, local_table)
    device_index = lax.axis_index("tensor")
    for section in range(tensor_count.bit_length() - 1):
        partner = partner_2(current.astype(jnp.bfloat16), "tensor", section).astype(current.dtype)
        high_half = jnp.right_shift(device_index, section) & 1 == 1
        current = jnp.where(high_half, partner - current, current + partner)
    grad_hidden = current * (1.0 / math.sqrt(tensor_count))
    grad_gate = (
        grad_hidden * up_vals * sigmoid_gate * (1.0 + gate_vals * (1.0 - sigmoid_gate))
    ).astype(jnp.bfloat16)
    grad_up = (grad_hidden * gate_vals * sigmoid_gate).astype(jnp.bfloat16)
    return (grad_gate, grad_up, grad_weight)


def solution(mesh):
    in_specs = (
        P("dp", "tensor"),
        P("dp", "tensor"),
        P("dp", "tensor"),
        P("dp", "tensor"),
        P("dp", "tensor"),
        P("tensor"),
        P("tensor"),
    )
    out_specs = (P("dp", "tensor"), P("dp", "tensor"), P("dp", "tensor"))
    return jax.shard_map(local, mesh=mesh, in_specs=in_specs, out_specs=out_specs, check_vma=False)
```

profile of v0, /device:TPU:1, one launch (start us, length us, event | category | flops | bytes accessed | tf_op | source)
XLA Modules:
  0.0 312.3 jit_solution(19975783899657542)
XLA Ops:
  7.2 0.0 all-gather.5.cloned.1.call-start
  7.2 0.7 all-gather.5.cloned.1.call-update
  7.9 1.3 copy.34
  9.2 0.1 reshape.256
  9.3 0.4 convolution_bitcast_fusion
  9.7 0.5 copy.36
  10.2 0.1 reshape.257
  10.3 0.0 copy-start
  10.3 0.0 copy-start.1
  10.4 4.5 %collective-permute-start = (bf16[128,1664]{0,1:T(8,128)(2,1)S(1)}, bf16[128,1664]{0,1:T(8,128)(2,1)S(1)}, u32[]{:S(2)}, u32[]{:S(2)}) collective-permute-start(bf16[128,1664]{0,1:T(8,128)(2,1)S(1)} %convert_element_type.75), channel_id=1, source_target_pairs={{0,1},{1,0},{2,3},{3,2},{4,5},{5,4},{6,7},{7,6},{8,9},{9,8},{10,11... | collective-permute-start | bytes 1277960 | tf_op jit(solution)/shard_map/ppermute | solution.py:15
  14.9 5.5 %collective-permute-done = bf16[128,1664]{0,1:T(8,128)(2,1)S(1)} collective-permute-done((bf16[128,1664]{0,1:T(8,128)(2,1)S(1)}, bf16[128,1664]{0,1:T(8,128)(2,1)S(1)}, u32[]{:S(2)}, u32[]{:S(2)}) %collective-permute-start) | collective-permute-done | bytes 426016 | tf_op jit(solution)/shard_map/ppermute | solution.py:15
  20.4 0.1 fusion.55
  20.5 8.8 %collective-permute-start.1 = (bf16[128,1664]{0,1:T(8,128)(2,1)S(1)}, bf16[128,1664]{0,1:T(8,128)(2,1)}, u32[]{:S(2)}, u32[]{:S(2)}) collective-permute-start(bf16[128,1664]{0,1:T(8,128)(2,1)S(1)} %fusion.55), channel_id=1, source_target_pairs={{0,2},{1,3},{2,0},{3,1},{4,6},{5,7},{6,4},{7,5},{8,10},{9,11},{10,... | collective-permute-start | bytes 1277960 | tf_op jit(solution)/shard_map/ppermute | solution.py:15
  29.4 18.5 %collective-permute-done.1 = bf16[128,1664]{0,1:T(8,128)(2,1)} collective-permute-done((bf16[128,1664]{0,1:T(8,128)(2,1)S(1)}, bf16[128,1664]{0,1:T(8,128)(2,1)}, u32[]{:S(2)}, u32[]{:S(2)}) %collective-permute-start.1) | collective-permute-done | bytes 426016 | tf_op jit(solution)/shard_map/ppermute | solution.py:15
  47.8 1.3 fusion.89
  49.1 8.8 %collective-permute-start.2 = (bf16[128,1664]{0,1:T(8,128)(2,1)S(1)}, bf16[128,1664]{0,1:T(8,128)(2,1)S(1)}, u32[]{:S(2)}, u32[]{:S(2)}) collective-permute-start(bf16[128,1664]{0,1:T(8,128)(2,1)S(1)} %get-tuple-element.12), channel_id=1, source_target_pairs={{0,4},{1,5},{2,6},{3,7},{4,0},{5,1},{6,2},{7,3},{8,12},{9,13},{10,... | collective-permute-start | bytes 1277960 | tf_op jit(solution)/shard_map/ppermute | solution.py:15
  57.9 36.5 %collective-permute-done.2 = bf16[128,1664]{0,1:T(8,128)(2,1)S(1)} collective-permute-done((bf16[128,1664]{0,1:T(8,128)(2,1)S(1)}, bf16[128,1664]{0,1:T(8,128)(2,1)S(1)}, u32[]{:S(2)}, u32[]{:S(2)}) %collective-permute-start.2) | collective-permute-done | bytes 426016 | tf_op jit(solution)/shard_map/ppermute | solution.py:15
  94.4 0.1 fusion.54
  94.6 22.2 %collective-permute-start.3 = (bf16[128,1664]{0,1:T(8,128)(2,1)S(1)}, bf16[128,1664]{0,1:T(8,128)(2,1)}, u32[]{:S(2)}, u32[]{:S(2)}) collective-permute-start(bf16[128,1664]{0,1:T(8,128)(2,1)S(1)} %fusion.54), channel_id=1, source_target_pairs={{0,8},{1,9},{2,10},{3,11},{4,12},{5,13},{6,14},{7,15},{8,0},{9,1},... | collective-permute-start | bytes 1277960 | tf_op jit(solution)/shard_map/ppermute | solution.py:15
  116.8 0.0 copy-done
  116.8 0.3 copy.38
  117.0 0.0 copy-done.1
  117.0 0.3 copy.37
  117.3 14.5 %collective-permute-done.3 = bf16[128,1664]{0,1:T(8,128)(2,1)} collective-permute-done((bf16[128,1664]{0,1:T(8,128)(2,1)S(1)}, bf16[128,1664]{0,1:T(8,128)(2,1)}, u32[]{:S(2)}, u32[]{:S(2)}) %collective-permute-start.3) | collective-permute-done | bytes 426016 | tf_op jit(solution)/shard_map/ppermute | solution.py:15
  131.8 1.8 fusion.53
  133.6 1.0 copy.39
  134.6 17.9 %all-to-all-start = ((bf16[16,8,1664]{2,1,0:T(8,128)(2,1)}), bf16[16,8,1664]{2,1,0:T(8,128)(2,1)S(1)}, u32[]{:S(2)}, u32[]{:S(2)}) async-start(bf16[16,8,1664]{2,1,0:T(8,128)(2,1)} %bitcast.3), calls=%async_computation | async-start | bytes 851968 | tf_op jit(solution)/shard_map/all_to_all | solution.py:46
  152.5 0.0 all-gather.3.cloned.1.call-start
  152.6 6.5 %fusion.97 = bf16[1024,1024,1]{1,0,2:T(8,128)(2,1)} fusion(s32[1024]{0:T(1024)S(1)} %get-tuple-element.23, s32[1024]{0:T(1024)S(1)} %get-tuple-element.24, s32[1024]{0:T(1024)S(1)} %get-tuple-element.25, s32[1024]{0:T(1024)S(1)} %get-tuple-element.26, s32[1024]{0:T(1024)S(1)} %get-tuple-element.27, ...), kind=kLoop, calls=%fused_computation.9.clone.clone.clone.clone.clone.clone.1 | loop fusion | flops 36700160 | bytes 2138112 | tf_op jit(solution)/shard_map/tpk,qp->tqk/dot_general | solution.py:34
  159.1 11.7 %all-to-all-done = bf16[16,8,1664]{2,1,0:T(8,128)(2,1)S(1)} async-done(((bf16[16,8,1664]{2,1,0:T(8,128)(2,1)}), bf16[16,8,1664]{2,1,0:T(8,128)(2,1)S(1)}, u32[]{:S(2)}, u32[]{:S(2)}) %all-to-all-start) | async-done | bytes 426016 | tf_op jit(solution)/shard_map/all_to_all | solution.py:46
  170.8 5.4 %reshape.258 = bf16[8,1024,26]{2,1,0:T(8,128)(2,1)S(1)} reshape(bf16[8,16,1664]{2,1,0:T(8,128)(2,1)S(1)} %copy.40) | data formatting | bytes 851968 | tf_op jit(solution)/shard_map/reshape | solution.py:33
  176.2 2.4 fusion.36
  178.6 0.0 copy-start.2
  178.6 0.0 copy-start.3
  178.6 1.1 copy.42
  179.7 4.0 %convert_element_type.95 = bf16[8,32,832]{2,1,0:T(8,128)(2,1)S(1)} reshape(bf16[8,1024,26]{2,1,0:T(8,128)(2,1)S(1)} %copy.42) | data formatting | bytes 851968 | tf_op jit(solution)/shard_map/convert_element_type | solution.py:47
  183.7 0.1 copy.43
  183.8 25.0 %all_to_all.32 = bf16[8,32,832]{2,0,1:T(8,128)(2,1)} all-to-all(bf16[8,32,832]{2,0,1:T(8,128)(2,1)S(1)} %copy.43), channel_id=1, replica_groups=mesh['dp'=32,'tensor'=16] {'dp'}, dimensions={1} | all-to-all | bytes 851968 | tf_op jit(solution)/shard_map/all_to_all | solution.py:48
  208.8 0.0 all-gather.3.cloned.1.call-update
  208.8 0.0 copy-done.2
  208.8 0.0 copy-done.3
  208.9 1.0 copy.45
  209.8 1.0 copy.44
  210.8 0.0 all-gather.5.cloned.1.call-done
  210.8 85.5 %all-gather.3.cloned.1.call-done = bf16[4096,832]{1,0:T(8,128)(2,1)} async-done(((bf16[256,832]{1,0:T(8,128)(2,1)}), bf16[4096,832]{1,0:T(8,128)(2,1)}) %all-gather.3.cloned.1.call-update) | async-done | bytes 6815760 | tf_op jit(solution)/shard_map/all_gather | solution.py:54
  296.3 9.1 %select_convert_fusion = bf16[832,512]{1,0:T(8,128)(2,1)} fusion(bf16[832,512]{1,0:T(8,128)(2,1)} %param.11, bf16[4096,832]{1,0:T(8,128)(2,1)} %all-gather.3.cloned.1.call-done, bf16[4096,512]{1,0:T(8,128)(2,1)} %bitcast.37, f32[512]{0:T(512)S(1)} %multiply_multiply_fusion), kind=kOutput, calls=%fused_computation.35 | convolution fusion | flops 3491790848 | bytes 12716032 | tf_op jit(solution)/shard_map/dot_general | solution.py:53
  (11 shorter events, 0.1 us)
Async XLA Ops:
  7.2 203.7 %all-gather.5.cloned.1.call-start = ((), (), s32[]{:S(2)}) async-start(), calls=%async_computation.3 | async-start | bytes 4325376 | tf_op jit(solution)/shard_map/all_gather | solution.py:51
  10.3 106.5 %copy-start = (bf16[128,1664]{1,0:T(8,128)(2,1)S(1)}, bf16[128,1664]{1,0:T(8,128)(2,1)}, u32[]{:S(2)}) copy-start(bf16[128,1664]{1,0:T(8,128)(2,1)} %param.7) | copy-start | bytes 1277956
  10.3 106.7 %copy-start.1 = (bf16[128,1664]{1,0:T(8,128)(2,1)S(1)}, bf16[128,1664]{1,0:T(8,128)(2,1)}, u32[]{:S(2)}) copy-start(bf16[128,1664]{1,0:T(8,128)(2,1)} %param.8) | copy-start | bytes 1277956
  10.4 10.0 %collective-permute-start = (bf16[128,1664]{0,1:T(8,128)(2,1)S(1)}, bf16[128,1664]{0,1:T(8,128)(2,1)S(1)}, u32[]{:S(2)}, u32[]{:S(2)}) collective-permute-start(bf16[128,1664]{0,1:T(8,128)(2,1)S(1)} %convert_element_type.75), channel_id=1, source_target_pairs={{0,1},{1,0},{2,3},{3,2},{4,5},{5,4},{6,7},{7,6},{8,9},{9,8},{10,11... | collective-permute-start | bytes 1277960 | tf_op jit(solution)/shard_map/ppermute | solution.py:15
  20.5 27.3 %collective-permute-start.1 = (bf16[128,1664]{0,1:T(8,128)(2,1)S(1)}, bf16[128,1664]{0,1:T(8,128)(2,1)}, u32[]{:S(2)}, u32[]{:S(2)}) collective-permute-start(bf16[128,1664]{0,1:T(8,128)(2,1)S(1)} %fusion.55), channel_id=1, source_target_pairs={{0,2},{1,3},{2,0},{3,1},{4,6},{5,7},{6,4},{7,5},{8,10},{9,11},{10,... | collective-permute-start | bytes 1277960 | tf_op jit(solution)/shard_map/ppermute | solution.py:15
  49.1 45.4 %collective-permute-start.2 = (bf16[128,1664]{0,1:T(8,128)(2,1)S(1)}, bf16[128,1664]{0,1:T(8,128)(2,1)S(1)}, u32[]{:S(2)}, u32[]{:S(2)}) collective-permute-start(bf16[128,1664]{0,1:T(8,128)(2,1)S(1)} %get-tuple-element.12), channel_id=1, source_target_pairs={{0,4},{1,5},{2,6},{3,7},{4,0},{5,1},{6,2},{7,3},{8,12},{9,13},{10,... | collective-permute-start | bytes 1277960 | tf_op jit(solution)/shard_map/ppermute | solution.py:15
  94.6 37.3 %collective-permute-start.3 = (bf16[128,1664]{0,1:T(8,128)(2,1)S(1)}, bf16[128,1664]{0,1:T(8,128)(2,1)}, u32[]{:S(2)}, u32[]{:S(2)}) collective-permute-start(bf16[128,1664]{0,1:T(8,128)(2,1)S(1)} %fusion.54), channel_id=1, source_target_pairs={{0,8},{1,9},{2,10},{3,11},{4,12},{5,13},{6,14},{7,15},{8,0},{9,1},... | collective-permute-start | bytes 1277960 | tf_op jit(solution)/shard_map/ppermute | solution.py:15
  134.6 36.2 %all-to-all-start = ((bf16[16,8,1664]{2,1,0:T(8,128)(2,1)}), bf16[16,8,1664]{2,1,0:T(8,128)(2,1)S(1)}, u32[]{:S(2)}, u32[]{:S(2)}) async-start(bf16[16,8,1664]{2,1,0:T(8,128)(2,1)} %bitcast.3), calls=%async_computation | async-start | bytes 851968 | tf_op jit(solution)/shard_map/all_to_all | solution.py:46
  152.5 143.8 %all-gather.3.cloned.1.call-start = ((), (), s32[]{:S(2)}) async-start(), calls=%async_computation.2 | async-start | bytes 7798784 | tf_op jit(solution)/shard_map/all_gather | solution.py:54
  178.6 30.2 %copy-start.2 = (s32[512]{0:T(512)S(1)}, s32[512]{0:T(512)}, u32[]{:S(2)}) copy-start(s32[512]{0:T(512)} %param.13) | copy-start | bytes 6148
  178.6 30.2 %copy-start.3 = (s32[512]{0:T(512)S(1)}, s32[512]{0:T(512)}, u32[]{:S(2)}) copy-start(s32[512]{0:T(512)} %param.12) | copy-start | bytes 6148
Sparse Core Ops, SparseCore 0:
  11.1 70.2 all-gather.4
  209.0 87.3 all-gather.2
where the time goes:
time: 313 us; the launch traced here: 312 us
  waiting for transfers between devices  173 us (55%)
  starting transfers between devices  62.3 us (20%)
  blocking collectives  25 us (8%)
  local copies, waits for them, and re-layouts  16 us (5%)
  between operations  14.3 us (5%)
  matrix products  11.9 us (4%)
  other arithmetic  9.93 us (3%)
    all_gather x1, waiting for transfers between devices, local(): lax.all_gather(blocks, 'tensor', axis=0, tiled=True)  85.5 us
    ppermute x4, waiting for transfers between devices, partner_2(): return lax.ppermute(value, axis, pairs)  75 us
    ppermute x4, starting transfers between devices, partner_2(): return lax.ppermute(value, axis, pairs)  44.3 us
    all_to_all x1, blocking collectives, local(): lax.all_to_all(rotated, 'dp', split_axis=1, concat_axis=0, tiled=True)  25 us
    all_to_all x1, starting transfers between devices, local(): lax.all_to_all(hidden, 'tensor', split_axis=0, concat_axis=1, tiled=True)  17.9 us
    all_to_all x1, waiting for transfers between devices, local(): lax.all_to_all(hidden, 'tensor', split_axis=0, concat_axis=1, tiled=True)  11.7 us
    dot_general x1, matrix products, local(): lax.dot_general(lax.all_gather(blocks, 'tensor', axis=0, tiled=True), gra...  9.13 us
    dot_general x1, other arithmetic, apply_table(): jnp.einsum('tpk,qp->tqk', shaped, table_bf, preferred_element_type=jnp.fl...  6.51 us
  transfers between devices with their start and end apart: 7, of which 6 were waited for; matrix products, arithmetic and copies ran while one was open for 9% of the time, Pallas kernels for 0%

commit v1 on v0

v1 whole, which is shorter than its diff:
```python
import jax
import jax.numpy as jnp
import numpy as np
from jax import lax
from jax.experimental import pallas as pl
from jax.experimental.pallas import tpu as pltpu
from jax.sharding import PartitionSpec as P

HAD = 1024
NBLK = 26
MESH = pl.DeviceIdType.MESH
BF = jnp.bfloat16
F32 = jnp.float32

ZN = 16
XY = 16
TOK = 128
UN = 1664
COL = 32
HALF = 896


def local_table():
    table = np.array([[1.0]])
    for _ in range(6):
        table = np.block([[table, table], [table, -table]])
    return np.kron(table / 8.0, np.eye(NBLK)).astype(jnp.bfloat16)


def hint(value, multiple):
    return pl.multiple_of(value, multiple)


CHUNKS = ((0, 896), (896, 384), (1280, 384))
PIECES = (
    ((0, 0, 0, 896, 0), (1, 1, 768, 128, 0)),
    ((2, 1, 896, 384, 128),),
    ((3, 1, 1280, 384, 512),),
)


def rotate16(src, dst, first, width):
    def tile(t, carry):
        lanes = pl.ds(hint(t * 128, 128), 128)
        vals = [src[j, :, lanes].astype(F32) for j in range(16)]
        for bit in range(4):
            step = 1 << bit
            for j in range(16):
                if not j & step:
                    low, high = vals[j], vals[j | step]
                    vals[j], vals[j | step] = low + high, low - high
        for j in range(16):
            dst[j, :, lanes] = (vals[j] * 0.25).astype(BF)
        return carry

    lax.fori_loop(first // 128, (first + width) // 128, tile, 0)


def kernel(
    gate, up, grot, gout, bound, latent_hbm, table_hbm, gg, gu, gw,
    acts, outs, part, send, other, own, got, turned, landed, hid, fin, fturn, fback,
    bt, table, latent, flipped, load_sem, ring_s, ring_r, f_s, f_r, fb_s, fb_r, b_s, b_r, e_s, e_r, g_s, g_r, z_s, z_r,
):
    i = lax.axis_index("dp")
    z = lax.axis_index("tensor")
    c = i % 2
    xy = i // 2
    x, y = xy // 4, xy % 4
    k_me = z // 2
    active = z % 2 == c

    def remote(src, dst, ssem, rsem, dp, zz):
        return pltpu.make_async_remote_copy(
            src_ref=src, dst_ref=dst, send_sem=ssem, recv_sem=rsem,
            device_id=(dp, zz), device_id_type=MESH,
        )

    load_table = pltpu.make_async_copy(table_hbm, table, load_sem.at[0])
    load_latent = pltpu.make_async_copy(latent_hbm, latent, load_sem.at[1])
    load_table.start()
    load_latent.start()

    barrier = pltpu.get_barrier_semaphore()

    def hail_z(off, carry):
        pl.semaphore_signal(barrier, inc=1, device_id=(i, (z + off) % ZN), device_id_type=MESH)
        return carry

    def hail_xy(off, carry):
        pl.semaphore_signal(barrier, inc=1, device_id=((i + off) % 32, z), device_id_type=MESH)
        return carry

    lax.fori_loop(1, ZN, hail_z, 0)
    lax.fori_loop(1, 32, hail_xy, 0)

    def make_hidden(t, carry):
        lanes = pl.ds(hint(t * 128, 128), 128)
        g = gate[:, lanes].astype(F32)
        u = up[:, lanes].astype(F32)
        hid[:, lanes] = (g * jax.nn.sigmoid(g) * u).astype(BF)
        return carry

    for t in range(4):
        lanes = slice(128 * t, 128 * (t + 1))
        bt[lanes, :] = gout[:, lanes].astype(F32).T.astype(BF)
    lax.fori_loop(0, UN // 128, make_hidden, 0)
    pl.semaphore_wait(barrier, ZN - 1 + 31)

    def f_copy(k):
        rows = pl.ds(hint(16 * k, 16), 16)
        return remote(grot.at[rows, :], fin.at[z], f_s.at[k], f_r.at[z], i, 2 * k + c)

    def f_start(j, carry):
        k = (k_me + 4 + j) % 8

        @pl.when(2 * k + c != z)
        def _():
            f_copy(k).start()

        return carry

    lax.fori_loop(0, 3, f_start, 0)

    def b_copy(off):
        peer = (xy + off) % XY
        return remote(
            bt.at[pl.ds(hint(COL * peer, COL), COL), :],
            outs.at[pl.ds(hint(COL * z, COL), COL), pl.ds(hint(TOK * xy, TOK), TOK)],
            b_s.at[off], b_r.at[xy], 2 * peer + c, z,
        )

    def b_start(off, carry):
        b_copy(off).start()
        return carry

    lax.fori_loop(1, XY, b_start, 0)
    outs[pl.ds(hint(COL * z, COL), COL), pl.ds(hint(TOK * xy, TOK), TOK)] = bt[
        pl.ds(hint(COL * xy, COL), COL), :
    ]

    @pl.when(active)
    def _():
        fin[z] = grot[pl.ds(hint(16 * k_me, 16), 16), :]

    load_table.wait()
    mine = pl.ds(hint(TOK * xy, TOK), TOK)

    def turn_hidden(t, carry):
        lanes = pl.ds(hint(t * 256, 256), 256)
        acts[mine, lanes] = jnp.dot(hid[...], table[:, lanes], preferred_element_type=F32).astype(BF)
        return carry

    lax.fori_loop(0, UN // 256, turn_hidden, 0)
    acts[mine, UN - 128 :] = jnp.dot(
        hid[...], table[:, UN - 128 :], preferred_element_type=F32
    ).astype(BF)

    place = (4 * x + (x + y) % 4, 4 * y + (x + y) % 4, z)

    def block_of(r, n):
        major, minor = n // 4, (n % 4 + 3 * (n // 4)) % 4
        return (4 * major + minor, 4 * minor + major, n)[r]

    def ring_copy(r, d, s, u):
        n = place[r]
        origin = (n + 16 - s) % 16 if d == 0 else (n + s) % 16
        peer = (n + 1) % 16 if d == 0 else (n + 15) % 16
        blk = block_of(r, origin)
        if r < 2:
            ref = acts.at[pl.ds(hint(TOK * blk + 64 * r + 32 * u, 32), 32), :]
            dp, zz = 2 * block_of(r, peer) + c, z
        else:
            ref = outs.at[pl.ds(hint(COL * blk + 16 * u, 16), 16), :]
            dp, zz = i, peer
        return remote(ref, ref, ring_s.at[r, d, s, u], ring_r.at[r, d, s, u], dp, zz)

    def ring_wait(r, d, s, u):
        n = place[r]
        origin = (n + 15 - s) % 16 if d == 0 else (n + s + 1) % 16
        blk = block_of(r, origin)
        if r < 2:
            ref = acts.at[pl.ds(hint(TOK * blk + 64 * r + 32 * u, 32), 32), :]
        else:
            ref = outs.at[pl.ds(hint(COL * blk + 16 * u, 16), 16), :]
        src = (n + 15) % 16 if d == 0 else (n + 1) % 16
        dp, zz = (2 * block_of(r, src) + c, z) if r < 2 else (i, src)
        remote(ref, ref, ring_s.at[r, d, s, u], ring_r.at[r, d, s, u], dp, zz).wait_recv()

    for u in range(2):
        for r in range(2):
            for d in range(2):
                ring_copy(r, d, 0, u).start()

    def b_wait(off, carry):
        src = (xy + off) % XY
        ref = outs.at[pl.ds(hint(COL * z, COL), COL), pl.ds(hint(TOK * src, TOK), TOK)]
        remote(ref, ref, b_s.at[off], b_r.at[src], 2 * src + c, z).wait_recv()
        return carry

    lax.fori_loop(1, XY, b_wait, 0)
    for u in range(2):
        for d in range(2):
            ring_copy(2, d, 0, u).start()

    def ring_step(s, carry):
        for u in range(2):
            for r in (2, 0, 1):
                for d in range(2):
                    ring_wait(r, d, s - 1, u)
                    ring_copy(r, d, s, u).start()
        return carry

    def ring_step_f(s, carry):
        f_start(s + 2, 0)
        return ring_step(s, carry)

    lax.fori_loop(1, 6, ring_step_f, 0)
    ring_step(6, 0)
    for u in range(2):
        for r in (2, 0, 1):
            for d in range(2):
                ring_wait(r, d, 6, u)
                if u == d:
                    ring_copy(r, d, 7, u).start()
    for r in (2, 0, 1):
        for d in range(2):
            ring_wait(r, d, 7, d)

    def fb_copy(dest):
        return remote(
            fturn.at[dest], fback.at[pl.ds(hint(16 * k_me, 16), 16), :],
            fb_s.at[dest], fb_r.at[k_me], i, dest,
        )

    @pl.when(active)
    def _():
        def f_wait(off, carry):
            src = (z + off) % ZN
            remote(fin.at[src], fin.at[src], f_s.at[0], f_r.at[src], i, src).wait_recv()
            return carry

        lax.fori_loop(1, ZN, f_wait, 0)
        rotate16(fin, fturn, 0, UN)

        def fb_start(off, carry):
            fb_copy((z + 7 + off) % ZN).start()
            return carry

        lax.fori_loop(1, 9, fb_start, 0)

        def fb_start2(off, carry):
            fb_copy((z + off) % ZN).start()
            return carry

        lax.fori_loop(1, 8, fb_start2, 0)
        fback[pl.ds(hint(16 * k_me, 16), 16), :] = fturn[z]

    def product(lanes, width):
        tile = jnp.dot(outs[...], acts[:, lanes], preferred_element_type=F32)
        tile = tile.reshape(ZN, COL, width)
        part[:, :, lanes] = tile
        send[:, :, lanes] = tile.astype(BF)

    def product_chunk(q):
        first, width = CHUNKS[q]

        def product_tile(t, carry):
            product(pl.ds(hint(first + t * 256, 128), 256), 256)
            return carry

        lax.fori_loop(0, width // 256, product_tile, 0)
        if width % 256:
            product(pl.ds(first + width - 128, 128), 128)

    def swap(q):
        lanes = pl.ds(*CHUNKS[q])
        return remote(
            send.at[:, pl.ds(hint(16 * (1 - c), 16), 16), lanes], other.at[:, :, lanes],
            e_s.at[q], e_r.at[q], 2 * xy + 1 - c, z,
        )

    def g_copy(q, dest):
        lanes = pl.ds(*CHUNKS[q])
        return remote(
            own.at[dest, :, lanes], got.at[z, :, lanes], g_s.at[q, dest], g_r.at[q, z], i, dest
        )

    def share(q):
        lanes = pl.ds(*CHUNKS[q])
        swap(q).wait_recv()

        def add_send(off, carry):
            j = (z + 8 + off) % ZN
            own[j, :, lanes] = (
                part[j, pl.ds(hint(16 * c, 16), 16), lanes] + other[j, :, lanes].astype(F32)
            ).astype(BF)

            @pl.when(j != z)
            def _():
                g_copy(q, j).start()

            return carry

        lax.fori_loop(0, ZN, add_send, 0)
        got[z, :, lanes] = own[z, :, lanes]

    product_chunk(0)
    swap(0).start()
    product_chunk(1)
    swap(1).start()
    share(0)
    product_chunk(2)
    swap(2).start()
    share(1)
    share(2)

    def fb_wait(k, carry):
        @pl.when(2 * k + c != z)
        def _():
            ref = fback.at[pl.ds(hint(16 * k, 16), 16), :]
            remote(ref, ref, fb_s.at[0], fb_r.at[k], i, 2 * k + c).wait_recv()

        return carry

    lax.fori_loop(0, 8, fb_wait, 0)

    def finish(lanes):
        gh = jnp.dot(fback[...], table[:, lanes], preferred_element_type=F32)
        g = gate[:, lanes].astype(F32)
        u = up[:, lanes].astype(F32)
        sg = jax.nn.sigmoid(g)
        gg[:, lanes] = (gh * u * sg * (1.0 + g * (1.0 - sg))).astype(BF)
        gu[:, lanes] = (gh * g * sg).astype(BF)

    def finish_tile(t, carry):
        finish(pl.ds(hint(t * 256, 256), 256))
        return carry

    lax.fori_loop(0, UN // 256, finish_tile, 0)
    finish(pl.ds(UN - 128, 128))

    def z_copy(piece, peer):
        p, core, first, width, at = piece
        return remote(
            turned.at[peer, :, pl.ds(first, width)],
            landed.at[pl.ds(hint(COL * xy + 16 * c, 16), 16), pl.ds(at, width)],
            z_s.at[p, peer], z_r.at[p, i], 2 * peer + core, z,
        )

    def g_wait_chunk(q):
        lanes = pl.ds(*CHUNKS[q])

        def g_wait(off, carry):
            src = (z + off) % ZN
            ref = got.at[src, :, lanes]
            remote(ref, ref, g_s.at[q, src], g_r.at[q, src], i, src).wait_recv()
            return carry

        lax.fori_loop(1, ZN, g_wait, 0)

    def z_send(piece):
        p, core, first, width, at = piece

        def z_start(off, carry):
            z_copy(piece, (xy + off) % XY).start()
            return carry

        lax.fori_loop(1, XY, z_start, 0)

        @pl.when(c == core)
        def _():
            landed[pl.ds(hint(COL * xy + 16 * c, 16), 16), at : at + width] = turned[
                xy, :, first : first + width
            ]

        @pl.when(c != core)
        def _():
            z_copy(piece, xy).start()

    def z_take(piece):
        p, core, first, width, at = piece

        @pl.when(c == core)
        def _():
            def z_wait(off, carry):
                src = (i + off) % 32
                ref = landed.at[pl.ds(hint(16 * src, 16), 16), pl.ds(at, width)]
                remote(ref, ref, z_s.at[p, 0], z_r.at[p, src], src, z).wait_recv()
                return carry

            lax.fori_loop(1, 32, z_wait, 0)

            def flip(t, carry):
                lanes = pl.ds(hint(t * 128, 128), 128)
                flipped[lanes, :] = landed[:, lanes].astype(F32).T
                return carry

            lax.fori_loop(at // 128, (at + width) // 128, flip, 0)

    for q in range(3):
        g_wait_chunk(q)
        rotate16(got, turned, *CHUNKS[q])
        for piece in PIECES[q]:
            z_send(piece)
        if q:
            for piece in PIECES[q - 1]:
                z_take(piece)
    for piece in PIECES[2]:
        z_take(piece)

    load_latent.wait()
    limit = bound[...]

    def mask(t, carry):
        rows = pl.ds(hint(t * 64, 64), 64)
        value = flipped[pl.ds(hint(t * 64 + 64 * c, 64), 64), :]
        inside = jnp.abs(latent[rows, :].astype(F32)) <= limit
        gw[rows, :] = jnp.where(inside, value, 0.0).astype(BF)
        return carry

    lax.fori_loop(0, 13, mask, 0)

    def ring_sent(s, carry):
        for r in range(3):
            for d in range(2):
                for u in range(2):
                    ring_copy(r, d, s, u).wait_send()
        return carry

    lax.fori_loop(0, 7, ring_sent, 0)
    for r in range(3):
        for d in range(2):
            ring_copy(r, d, 7, d).wait_send()

    def f_sent(k, carry):
        @pl.when(2 * k + c != z)
        def _():
            f_copy(k).wait_send()

        return carry

    lax.fori_loop(0, 8, f_sent, 0)

    def b_sent(off, carry):
        b_copy(off).wait_send()
        return carry

    lax.fori_loop(1, XY, b_sent, 0)

    @pl.when(active)
    def _():
        def fb_sent(off, carry):
            fb_copy((z + off) % ZN).wait_send()
            return carry

        lax.fori_loop(1, ZN, fb_sent, 0)

    def g_sent(off, carry):
        for q in range(3):
            g_copy(q, (z + off) % ZN).wait_send()
        return carry

    lax.fori_loop(1, ZN, g_sent, 0)

    def z_sent(off, carry):
        for pieces in PIECES:
            for piece in pieces:
                z_copy(piece, (xy + off) % XY).wait_send()
        return carry

    lax.fori_loop(1, XY, z_sent, 0)
    for q in range(3):
        swap(q).wait_send()
        for piece in PIECES[q]:

            @pl.when(c != piece[1])
            def _():
                z_copy(piece, xy).wait_send()


def local(gate_pre, up_pre, grad_rot, grad_out, latent_weight, clip_codes, bits):
    table = jnp.asarray(local_table())
    vmem = pl.BlockSpec(memory_space=pltpu.VMEM)
    dma = pltpu.SemaphoreType.DMA
    hbm = pl.BlockSpec(memory_space=pl.ANY)
    levels = jnp.left_shift(jnp.int32(1), bits - 1) - 1
    clip_bound = clip_codes.astype(F32) * levels.astype(F32) / 65536.0
    return pl.pallas_call(
        kernel,
        out_shape=(
            jax.ShapeDtypeStruct((TOK, UN), BF),
            jax.ShapeDtypeStruct((TOK, UN), BF),
            jax.ShapeDtypeStruct((832, 512), BF),
        ),
        in_specs=[vmem] * 5 + [hbm] * 2,
        out_specs=(vmem, vmem, vmem),
        scratch_shapes=[
            pltpu.VMEM((XY * TOK, UN), BF),
            pltpu.VMEM((512, XY * TOK), BF),
            pltpu.VMEM((ZN, COL, UN), F32),
            pltpu.VMEM((ZN, COL, UN), BF),
            pltpu.VMEM((ZN, 16, UN), BF),
            pltpu.VMEM((ZN, 16, UN), BF),
            pltpu.VMEM((ZN, 16, UN), BF),
            pltpu.VMEM((ZN, 16, UN), BF),
            pltpu.VMEM((512, HALF), BF),
            pltpu.VMEM((TOK, UN), BF),
            pltpu.VMEM((ZN, 16, UN), BF),
            pltpu.VMEM((ZN, 16, UN), BF),
            pltpu.VMEM((TOK, UN), BF),
            pltpu.VMEM((512, TOK), BF),
            pltpu.VMEM((UN, UN), BF),
            pltpu.VMEM((832, 512), BF),
            pltpu.VMEM((HALF, 512), F32),
            dma((2,)),
            dma((3, 2, 8, 2)), dma((3, 2, 8, 2)),
            dma((8,)), dma((ZN,)), dma((ZN,)), dma((8,)),
            dma((XY,)), dma((XY,)), dma((3,)), dma((3,)),
            dma((3, ZN)), dma((3, ZN)), dma((4, XY)), dma((4, 32)),
        ],
        compiler_params=pltpu.CompilerParams(
            collective_id=0, has_side_effects=True, vmem_limit_bytes=56 * 1024 * 1024
        ),
    )(gate_pre, up_pre, grad_rot, grad_out, clip_bound[None, :], latent_weight, table)


def solution(mesh):
    both = P("dp", "tensor")
    return jax.shard_map(
        local,
        mesh=mesh,
        in_specs=(both, both, both, both, both, P("tensor"), P("tensor")),
        out_specs=(both, both, both),
        check_vma=False,
    )
```

time: 313 us -> 161 us (0.51)
  waiting for transfers between devices: 173 us -> 0 us
  Pallas kernels: 0 us -> 153 us
  starting transfers between devices: 62.3 us -> 0 us
  blocking collectives: 25 us -> 0 us
  between operations: 14.3 us -> 0.64 us
  matrix products: 11.9 us -> 0 us
  local copies, waits for them, and re-layouts: 16 us -> 5.7 us
  other arithmetic: 9.93 us -> 1.28 us
    pallas_call x0 -> x1, Pallas kernels: none -> 153 us  [local(): pl.pallas_call(kernel, out_shape=(jax.ShapeDtypeStruct((TOK, UN), BF), ja...]
    all_gather x2 -> x0, waiting for transfers between devices: 85.5 us -> none  [the longest x1 85.5 us: local(): lax.all_gather(blocks, 'tensor', axis=0, tiled=True)]
    ppermute x4 -> x0, waiting for transfers between devices: 75 us -> none  [partner_2(): return lax.ppermute(value, axis, pairs)]
    ppermute x4 -> x0, starting transfers between devices: 44.3 us -> none  [partner_2(): return lax.ppermute(value, axis, pairs)]
    all_to_all x1 -> x0, blocking collectives: 25 us -> none  [local(): lax.all_to_all(rotated, 'dp', split_axis=1, concat_axis=0, tiled=True)]
    all_to_all x1 -> x0, starting transfers between devices: 17.9 us -> none  [local(): lax.all_to_all(hidden, 'tensor', split_axis=0, concat_axis=1, tiled=True)]
    dot_general x3 -> x0, matrix products: 11.9 us -> none  [the longest x1 9.13 us: local(): lax.dot_general(lax.all_gather(blocks, 'tensor', axis=0, tiled=True), gra...]
    all_to_all x1 -> x0, waiting for transfers between devices: 11.7 us -> none  [local(): lax.all_to_all(hidden, 'tensor', split_axis=0, concat_axis=1, tiled=True)]
  transfers between devices with their start and end apart: 7 -> 0, of which waited for: 6 -> 0; matrix products, arithmetic and copies ran while one was open for 9% -> 0% of each run, Pallas kernels for 0% -> 0%
where the time goes in v1:
time: 161 us
  Pallas kernels  153 us (95%)
  local copies, waits for them, and re-layouts  5.7 us (4%)
    pallas_call x1, Pallas kernels, local(): pl.pallas_call(kernel, out_shape=(jax.ShapeDtypeStruct((TOK, UN), BF), ja...  153 us
    unnamed x3, local copies, waits for them, and re-layouts  5.7 us

profile of v1, /device:TPU:1, one launch (start us, length us, event | category | flops | bytes accessed | tf_op | source)
XLA Modules:
  0.0 160.6 jit_solution(5154116786527848647)
XLA Ops:
  0.6 1.3 multiply_multiply_fusion
  1.9 153.0 %shard_map.103 = (bf16[128,1664]{1,0:T(8,128)(2,1)}, bf16[128,1664]{1,0:T(8,128)(2,1)}, bf16[832,512]{1,0:T(8,128)(2,1)}) custom-call(bf16[128,1664]{1,0:T(8,128)(2,1)} %gate.1, bf16[128,1664]{1,0:T(8,128)(2,1)} %up.1, bf16[128,1664]{1,0:T(8,128)(2,1)} %grot.1, bf16[128,512]{1,0:T(8,128)(2,1)} %gout.1, f32[1,512]{1,0:T(1,128)} %bitcast.1, ...), custom_call_target="tpu_custom_call" | custom-call | tf_op jit(solution)/shard_map/pallas_call | solution.py:488
  154.9 1.8 %copy.14 = bf16[128,1664]{1,0:T(8,128)(2,1)} copy(bf16[128,1664]{1,0:T(8,128)(2,1)} %get-tuple-element.6) | data formatting | bytes 851968
  156.7 1.8 %copy.15 = bf16[128,1664]{1,0:T(8,128)(2,1)} copy(bf16[128,1664]{1,0:T(8,128)(2,1)} %get-tuple-element.7) | data formatting | bytes 851968
  158.5 2.1 %copy.16 = bf16[832,512]{1,0:T(8,128)(2,1)} copy(bf16[832,512]{1,0:T(8,128)(2,1)} %get-tuple-element.8) | data formatting | bytes 1703936

commit v2 on v1

v2 whole, which is shorter than its diff:
```python
import jax
import jax.numpy as jnp
import numpy as np
from jax import lax
from jax.experimental import pallas as pl
from jax.experimental.pallas import tpu as pltpu
from jax.sharding import PartitionSpec as P

HAD = 1024
NBLK = 26
MESH = pl.DeviceIdType.MESH
BF = jnp.bfloat16
F32 = jnp.float32

ZN = 16
XY = 16
TOK = 128
UN = 1664
COL = 32
HALF = 896


def local_table():
    table = np.array([[1.0]])
    for _ in range(6):
        table = np.block([[table, table], [table, -table]])
    return np.kron(table / 8.0, np.eye(NBLK)).astype(jnp.bfloat16)


def hint(value, multiple):
    return pl.multiple_of(value, multiple)


CHUNKS = ((0, 896), (896, 384), (1280, 384))
PIECES = (
    ((0, 0, 0, 896, 0), (1, 1, 768, 128, 0)),
    ((2, 1, 896, 384, 128),),
    ((3, 1, 1280, 384, 512),),
)


def rotate16(src, dst, first, width):
    def tile(t, carry):
        lanes = pl.ds(hint(t * 128, 128), 128)
        vals = [src[j, :, lanes].astype(F32) for j in range(16)]
        for bit in range(4):
            step = 1 << bit
            for j in range(16):
                if not j & step:
                    low, high = vals[j], vals[j | step]
                    vals[j], vals[j | step] = low + high, low - high
        for j in range(16):
            dst[j, :, lanes] = (vals[j] * 0.25).astype(BF)
        return carry

    lax.fori_loop(first // 128, (first + width) // 128, tile, 0)


def kernel(
    gate, up, grot, gout, table_hbm, gh_out, gw_out,
    acts, outs, part, send, other, own, got, turned, landed, hid, fin, fturn, fback,
    bt, table, load_sem, ring_s, ring_r, f_s, f_r, fb_s, fb_r, b_s, b_r, e_s, e_r, g_s, g_r, z_s, z_r,
):
    i = lax.axis_index("dp")
    z = lax.axis_index("tensor")
    c = i & 1
    xy = i >> 1
    x, y = xy >> 2, xy & 3
    k_me = z >> 1
    active = (z & 1) == c

    def remote(src, dst, ssem, rsem, dp, zz):
        return pltpu.make_async_remote_copy(
            src_ref=src, dst_ref=dst, send_sem=ssem, recv_sem=rsem,
            device_id=(dp, zz), device_id_type=MESH,
        )

    load_table = pltpu.make_async_copy(table_hbm, table, load_sem)
    load_table.start()

    def taken(ref, sem):
        remote(ref, ref, load_sem, sem, i, z ^ 1).wait_recv()

    def gone(ref, sem):
        remote(ref, ref, sem, load_sem, i, z ^ 1).wait_send()

    barrier = pltpu.get_barrier_semaphore()

    def hail_z(off, carry):
        pl.semaphore_signal(barrier, inc=1, device_id=(i, (z + off) & 15), device_id_type=MESH)
        return carry

    def hail_xy(off, carry):
        pl.semaphore_signal(barrier, inc=1, device_id=((i + off) & 31, z), device_id_type=MESH)
        return carry

    lax.fori_loop(1, ZN, hail_z, 0)
    lax.fori_loop(1, 32, hail_xy, 0)

    def make_hidden(t, carry):
        lanes = pl.ds(hint(t * 128, 128), 128)
        g = gate[:, lanes].astype(F32)
        u = up[:, lanes].astype(F32)
        hid[:, lanes] = (g * jax.nn.sigmoid(g) * u).astype(BF)
        return carry

    for t in range(4):
        lanes = slice(128 * t, 128 * (t + 1))
        bt[lanes, :] = gout[:, lanes].astype(F32).T.astype(BF)
    lax.fori_loop(0, UN // 128, make_hidden, 0)
    pl.semaphore_wait(barrier, ZN - 1 + 31)

    def f_copy(k):
        rows = pl.ds(hint(16 * k, 16), 16)
        return remote(grot.at[rows, :], fin.at[z], f_s, f_r, i, 2 * k + c)

    def f_start(j, carry):
        k = (k_me + 4 + j) & 7

        @pl.when(2 * k + c != z)
        def _():
            f_copy(k).start()

        return carry

    lax.fori_loop(0, 3, f_start, 0)

    def b_copy(off):
        peer = (xy + off) & 15
        return remote(
            bt.at[pl.ds(hint(COL * peer, COL), COL), :],
            outs.at[pl.ds(hint(COL * z, COL), COL), pl.ds(hint(TOK * xy, TOK), TOK)],
            b_s, b_r, 2 * peer + c, z,
        )

    def b_start(off, carry):
        b_copy(off).start()
        return carry

    lax.fori_loop(1, XY, b_start, 0)
    outs[pl.ds(hint(COL * z, COL), COL), pl.ds(hint(TOK * xy, TOK), TOK)] = bt[
        pl.ds(hint(COL * xy, COL), COL), :
    ]

    @pl.when(active)
    def _():
        fin[z] = grot[pl.ds(hint(16 * k_me, 16), 16), :]

    load_table.wait()
    mine = pl.ds(hint(TOK * xy, TOK), TOK)

    def turn_hidden(t, carry):
        lanes = pl.ds(hint(t * 256, 256), 256)
        acts[mine, lanes] = jnp.dot(hid[...], table[:, lanes], preferred_element_type=F32).astype(BF)
        return carry

    lax.fori_loop(0, UN // 256, turn_hidden, 0)
    acts[mine, UN - 128 :] = jnp.dot(
        hid[...], table[:, UN - 128 :], preferred_element_type=F32
    ).astype(BF)

    place = (4 * x + ((x + y) & 3), 4 * y + ((x + y) & 3), z)

    def block_of(r, n):
        if r == 2:
            return n
        major = n >> 2
        minor = (n + 3 * major) & 3
        return 4 * major + minor if r == 0 else 4 * minor + major

    def ring_peer(r, n):
        return (i, n) if r == 2 else (2 * block_of(r, n) + c, z)

    peers = [[ring_peer(r, (place[r] + hop) & 15) for hop in (1, 15)] for r in range(3)]

    def ring_copy(r, d, s, u):
        blk = block_of(r, (place[r] + 16 - s if d == 0 else place[r] + s) & 15)
        if r < 2:
            ref = acts.at[pl.ds(hint(TOK * blk + 64 * r + 32 * u, 32), 32), :]
        else:
            ref = outs.at[pl.ds(hint(COL * blk + 16 * u, 16), 16), :]
        return remote(ref, ref, ring_s.at[r], ring_r.at[r, d, s, u], *peers[r][d])

    def ring_wait(r, d, s, u):
        taken(acts.at[pl.ds(0, 32), :] if r < 2 else outs.at[pl.ds(0, 16), :], ring_r.at[r, d, s, u])

    for u in range(2):
        for r in range(2):
            for d in range(2):
                ring_copy(r, d, 0, u).start()

    taken(outs.at[pl.ds(0, COL), pl.ds(0, TOK * (XY - 1))], b_r)
    for u in range(2):
        for d in range(2):
            ring_copy(2, d, 0, u).start()

    def ring_step(s, carry):
        for u in range(2):
            for r in (2, 0, 1):
                for d in range(2):
                    ring_wait(r, d, s - 1, u)
                    ring_copy(r, d, s, u).start()
        return carry

    def ring_step_f(s, carry):
        f_start(s + 2, 0)
        return ring_step(s, carry)

    lax.fori_loop(1, 6, ring_step_f, 0)
    ring_step(6, 0)
    for u in range(2):
        for r in (2, 0, 1):
            for d in range(2):
                ring_wait(r, d, 6, u)
                if u == d:
                    ring_copy(r, d, 7, u).start()
    for r in (2, 0, 1):
        for d in range(2):
            ring_wait(r, d, 7, d)

    def fb_copy(dest):
        return remote(
            fturn.at[dest], fback.at[pl.ds(hint(16 * k_me, 16), 16), :],
            fb_s, fb_r, i, dest,
        )

    @pl.when(active)
    def _():
        taken(fin.at[pl.ds(0, ZN - 1)], f_r)
        rotate16(fin, fturn, 0, UN)

        def fb_start(off, carry):
            fb_copy((z + 7 + off) & 15).start()
            return carry

        lax.fori_loop(1, 9, fb_start, 0)

        def fb_start2(off, carry):
            fb_copy((z + off) & 15).start()
            return carry

        lax.fori_loop(1, 8, fb_start2, 0)
        fback[pl.ds(hint(16 * k_me, 16), 16), :] = fturn[z]

    def product(lanes, width):
        tile = jnp.dot(outs[...], acts[:, lanes], preferred_element_type=F32)
        tile = tile.reshape(ZN, COL, width)
        part[:, :, lanes] = tile
        send[:, :, lanes] = tile.astype(BF)

    def product_chunk(q):
        first, width = CHUNKS[q]

        def product_tile(t, carry):
            product(pl.ds(hint(first + t * 256, 128), 256), 256)
            return carry

        lax.fori_loop(0, width // 256, product_tile, 0)
        if width % 256:
            product(pl.ds(first + width - 128, 128), 128)

    def swap(q):
        lanes = pl.ds(*CHUNKS[q])
        return remote(
            send.at[:, pl.ds(hint(16 * (1 - c), 16), 16), lanes], other.at[:, :, lanes],
            e_s, e_r.at[q], i ^ 1, z,
        )

    def g_copy(q, dest):
        lanes = pl.ds(*CHUNKS[q])
        return remote(
            own.at[dest, :, lanes], got.at[z, :, lanes], g_s, g_r.at[q], i, dest
        )

    def share(q):
        lanes = pl.ds(*CHUNKS[q])
        taken(other.at[:, :, lanes], e_r.at[q])

        def add_send(off, carry):
            j = (z + 8 + off) & 15
            own[j, :, lanes] = (
                part[j, pl.ds(hint(16 * c, 16), 16), lanes] + other[j, :, lanes].astype(F32)
            ).astype(BF)

            @pl.when(j != z)
            def _():
                g_copy(q, j).start()

            return carry

        lax.fori_loop(0, ZN, add_send, 0)
        got[z, :, lanes] = own[z, :, lanes]

    product_chunk(0)
    swap(0).start()
    product_chunk(1)
    swap(1).start()
    share(0)
    product_chunk(2)
    swap(2).start()
    share(1)
    share(2)

    @pl.when(active)
    def _():
        taken(fback.at[pl.ds(0, TOK - 16), :], fb_r)

    @pl.when(jnp.logical_not(active))
    def _():
        taken(fback, fb_r)

    def finish(lanes):
        gh_out[:, lanes] = jnp.dot(fback[...], table[:, lanes], preferred_element_type=F32).astype(BF)

    def finish_tile(t, carry):
        finish(pl.ds(hint(t * 256, 256), 256))
        return carry

    lax.fori_loop(0, UN // 256, finish_tile, 0)
    finish(pl.ds(UN - 128, 128))

    def z_copy(piece, peer):
        p, core, first, width, at = piece
        return remote(
            turned.at[peer, :, pl.ds(first, width)],
            landed.at[pl.ds(hint(COL * xy + 16 * c, 16), 16), pl.ds(at, width)],
            z_s.at[p], z_r.at[p], 2 * peer + core, z,
        )

    def g_wait_chunk(q):
        lanes = pl.ds(*CHUNKS[q])

        taken(got.at[pl.ds(0, ZN - 1), :, lanes], g_r.at[q])

    def z_send(piece):
        p, core, first, width, at = piece

        def z_start(off, carry):
            z_copy(piece, (xy + off) & 15).start()
            return carry

        lax.fori_loop(1, XY, z_start, 0)

        @pl.when(c == core)
        def _():
            landed[pl.ds(hint(COL * xy + 16 * c, 16), 16), at : at + width] = turned[
                xy, :, first : first + width
            ]

        @pl.when(c != core)
        def _():
            z_copy(piece, xy).start()

    def z_take(piece):
        p, core, first, width, at = piece

        @pl.when(c == core)
        def _():
            taken(landed.at[pl.ds(0, 496), pl.ds(at, width)], z_r.at[p])

            def flip(t, carry):
                lanes = pl.ds(hint(t * 128, 128), 128)
                gw_out[lanes, :] = landed[:, lanes].astype(F32).T.astype(BF)
                return carry

            lax.fori_loop(at // 128, (at + width) // 128, flip, 0)

    for q in range(3):
        g_wait_chunk(q)
        rotate16(got, turned, *CHUNKS[q])
        for piece in PIECES[q]:
            z_send(piece)
        if q:
            for piece in PIECES[q - 1]:
                z_take(piece)
    for piece in PIECES[2]:
        z_take(piece)

    for r in range(2):
        gone(acts.at[pl.ds(0, 64 * 15), :], ring_s.at[r])
    gone(outs.at[pl.ds(0, COL * 15), :], ring_s.at[2])
    gone(outs.at[pl.ds(0, COL), pl.ds(0, TOK * (XY - 1))], b_s)

    @pl.when(active)
    def _():
        gone(grot.at[pl.ds(0, TOK - 16), :], f_s)
        gone(fturn.at[pl.ds(0, ZN - 1)], fb_s)

    @pl.when(jnp.logical_not(active))
    def _():
        gone(grot, f_s)

    gone(other, e_s)
    gone(own.at[pl.ds(0, ZN - 1)], g_s)
    for pieces in PIECES:
        for p, core, first, width, at in pieces:

            @pl.when(c == core)
            def _():
                gone(turned.at[pl.ds(0, XY - 1), :, pl.ds(first, width)], z_s.at[p])

            @pl.when(c != core)
            def _():
                gone(turned.at[:, :, pl.ds(first, width)], z_s.at[p])


def local(gate_pre, up_pre, grad_rot, grad_out, latent_weight, clip_codes, bits):
    table = jnp.asarray(local_table())
    vmem = pl.BlockSpec(memory_space=pltpu.VMEM)
    hbm = pl.BlockSpec(memory_space=pl.ANY)
    dma = pltpu.SemaphoreType.DMA
    grad_hidden, summed = pl.pallas_call(
        kernel,
        out_shape=(
            jax.ShapeDtypeStruct((TOK, UN), BF),
            jax.ShapeDtypeStruct((HALF, 512), BF),
        ),
        in_specs=[vmem] * 4 + [hbm],
        out_specs=(vmem, vmem),
        scratch_shapes=[
            pltpu.VMEM((XY * TOK, UN), BF),
            pltpu.VMEM((512, XY * TOK), BF),
            pltpu.VMEM((ZN, COL, UN), F32),
            pltpu.VMEM((ZN, COL, UN), BF),
            pltpu.VMEM((ZN, 16, UN), BF),
            pltpu.VMEM((ZN, 16, UN), BF),
            pltpu.VMEM((ZN, 16, UN), BF),
            pltpu.VMEM((ZN, 16, UN), BF),
            pltpu.VMEM((512, HALF), BF),
            pltpu.VMEM((TOK, UN), BF),
            pltpu.VMEM((ZN, 16, UN), BF),
            pltpu.VMEM((ZN, 16, UN), BF),
            pltpu.VMEM((TOK, UN), BF),
            pltpu.VMEM((512, TOK), BF),
            pltpu.VMEM((UN, UN), BF),
            dma(()), dma((3,)), dma((3, 2, 8, 2)),
            dma(()), dma(()), dma(()), dma(()),
            dma(()), dma(()), dma(()), dma((3,)),
            dma(()), dma((3,)), dma((4,)), dma((4,)),
        ],
        compiler_params=pltpu.CompilerParams(
            collective_id=0, has_side_effects=True, vmem_limit_bytes=56 * 1024 * 1024
        ),
    )(gate_pre, up_pre, grad_rot, grad_out, table)
    core = lax.axis_index("dp") & 1
    rows = jnp.where(core == 1, summed[HALF - 832 :], summed[:832])
    levels = jnp.left_shift(jnp.int32(1), bits - 1) - 1
    clip_bound = clip_codes.astype(F32) * levels.astype(F32) / 65536.0
    inside = jnp.abs(latent_weight.astype(F32)) <= clip_bound[None, :]
    grad_weight = jnp.where(inside, rows, jnp.zeros((), BF))
    gate_vals, up_vals = gate_pre.astype(F32), up_pre.astype(F32)
    gh = grad_hidden.astype(F32)
    sg = jax.nn.sigmoid(gate_vals)
    grad_gate = (gh * up_vals * sg * (1.0 + gate_vals * (1.0 - sg))).astype(BF)
    grad_up = (gh * gate_vals * sg).astype(BF)
    return grad_gate, grad_up, grad_weight


def solution(mesh):
    both = P("dp", "tensor")
    return jax.shard_map(
        local,
        mesh=mesh,
        in_specs=(both, both, both, both, both, P("tensor"), P("tensor")),
        out_specs=(both, both, both),
        check_vma=False,
    )
```

time: 161 us -> 153 us (0.950)
  Pallas kernels: 153 us -> 147 us
  local copies, waits for them, and re-layouts: 5.7 us -> 0.02 us
  other arithmetic: 1.28 us -> 4.52 us
    unnamed x3 -> x8, local copies, waits for them, and re-layouts: 5.7 us -> 0.02 us
    pallas_call x1, Pallas kernels: 153 us -> 147 us  [local(): pl.pallas_call(kernel, out_shape=(jax.ShapeDtypeStruct((TOK, UN), BF), ja...]
    convert_element_type x0 -> x1, other arithmetic: none -> 2.48 us  [local(): grad_up = (gh * gate_vals * sg).astype(BF)]
where the time goes in v2:
time: 153 us
  Pallas kernels  147 us (96%)
  other arithmetic  4.52 us (3%)
    pallas_call x1, Pallas kernels, local(): pl.pallas_call(kernel, out_shape=(jax.ShapeDtypeStruct((TOK, UN), BF), ja...  147 us

profile of v2, /device:TPU:1, one launch (start us, length us, event | category | flops | bytes accessed | tf_op | source)
XLA Modules:
  0.0 152.6 jit_solution(7493240731940636217)
XLA Ops:
  0.6 0.7 multiply_multiply_fusion
  1.3 0.0 copy-start.1
  1.3 0.0 copy-start.2
  1.3 147.4 %shard_map.103 = (bf16[128,1664]{1,0:T(8,128)(2,1)}, bf16[896,512]{1,0:T(8,128)(2,1)}) custom-call(bf16[128,1664]{1,0:T(8,128)(2,1)} %gate.1, bf16[128,1664]{1,0:T(8,128)(2,1)} %up.1, bf16[128,1664]{1,0:T(8,128)(2,1)} %grot.1, bf16[128,512]{1,0:T(8,128)(2,1)} %gout.1, bf16[1664,1664]{1,0:T(8,128)(2,1)} %constant.21.clone.table_hbm), custom_call_target="tpu_custom_call" | custom-call | tf_op jit(solution)/shard_map/pallas_call | solution.py:412
  148.7 0.0 copy-start
  148.7 0.0 copy-start.3
  148.7 0.0 copy-done.1
  148.7 0.0 copy-done.2
  148.8 2.5 %fusion.9 = (bf16[128,1664]{1,0:T(8,128)(2,1)}, bf16[128,1664]{1,0:T(8,128)(2,1)}) fusion(bf16[128,1664]{1,0:T(8,128)(2,1)S(1)} %copy-done.1, bf16[128,1664]{1,0:T(8,128)(2,1)} %get-tuple-element.5, bf16[128,1664]{1,0:T(8,128)(2,1)S(1)} %copy-done.2), kind=kLoop, calls=%fused_computation.14 | loop fusion | flops 3407872 | bytes 2129920 | tf_op jit(solution)/shard_map/convert_element_type | solution.py:455
  151.2 0.0 copy-done
  151.2 0.0 copy-done.3
  151.2 1.3 fusion
Async XLA Ops:
  1.3 147.4 %copy-start.1 = (bf16[128,1664]{1,0:T(8,128)(2,1)S(1)}, bf16[128,1664]{1,0:T(8,128)(2,1)}, u32[]{:S(2)}) copy-start(bf16[128,1664]{1,0:T(8,128)(2,1)} %gate.1) | copy-start | bytes 1277956
  1.3 147.4 %copy-start.2 = (bf16[128,1664]{1,0:T(8,128)(2,1)S(1)}, bf16[128,1664]{1,0:T(8,128)(2,1)}, u32[]{:S(2)}) copy-start(bf16[128,1664]{1,0:T(8,128)(2,1)} %up.1) | copy-start | bytes 1277956
  148.7 2.5 %copy-start = (bf16[896,512]{1,0:T(8,128)(2,1)S(1)}, bf16[896,512]{1,0:T(8,128)(2,1)}, u32[]{:S(2)}) copy-start(bf16[896,512]{1,0:T(8,128)(2,1)} %get-tuple-element.6) | copy-start | bytes 2752516
  148.7 2.5 %copy-start.3 = (bf16[832,512]{1,0:T(8,128)(2,1)S(1)}, bf16[832,512]{1,0:T(8,128)(2,1)}, u32[]{:S(2)}) copy-start(bf16[832,512]{1,0:T(8,128)(2,1)} %param.12) | copy-start | bytes 2555908

commit v3 on v2

--- a/solution.py
+++ b/solution.py
@@ -37,6 +37,11 @@
     ((2, 1, 896, 384, 128),),
     ((3, 1, 1280, 384, 512),),
 )
+
+
+def far_first(t):
+    half = (t + 1) >> 1
+    return (8 + half * (1 - 2 * (t & 1))) & 15
 
 
 def rotate16(src, dst, first, width):
@@ -97,6 +102,48 @@
     lax.fori_loop(1, ZN, hail_z, 0)
     lax.fori_loop(1, 32, hail_xy, 0)
 
+    for t in range(4):
+        lanes = slice(128 * t, 128 * (t + 1))
+        bt[lanes, :] = gout[:, lanes].astype(F32).T.astype(BF)
+    pl.semaphore_wait(barrier, ZN - 1 + 31)
+
+    def f_copy(k):
+        rows = pl.ds(hint(16 * k, 16), 16)
+        return remote(grot.at[rows, :], fin.at[z], f_s, f_r, i, 2 * k + c)
+
+    def f_start(j, carry):
+        half = (j + 1) >> 1
+        k = (k_me + 4 + half * (1 - 2 * (j & 1))) & 7
+
+        @pl.when(2 * k + c != z)
+        def _():
+            f_copy(k).start()
+
+        return carry
+
+    lax.fori_loop(0, 3, f_start, 0)
+
+    def b_copy(off):
+        peer = (xy + 7 * off) & 15
+        return remote(
+            bt.at[pl.ds(hint(COL * peer, COL), COL), :],
+            outs.at[pl.ds(hint(COL * z, COL), COL), pl.ds(hint(TOK * xy, TOK), TOK)],
+            b_s, b_r, 2 * peer + c, z,
+        )
+
+    def b_start(off, carry):
+        b_copy(off).start()
+        return carry
+
+    lax.fori_loop(1, XY, b_start, 0)
+    outs[pl.ds(hint(COL * z, COL), COL), pl.ds(hint(TOK * xy, TOK), TOK)] = bt[
+        pl.ds(hint(COL * xy, COL), COL), :
+    ]
+
+    @pl.when(active)
+    def _():
+        fin[z] = grot[pl.ds(hint(16 * k_me, 16), 16), :]
+
     def make_hidden(t, carry):
         lanes = pl.ds(hint(t * 128, 128), 128)
         g = gate[:, lanes].astype(F32)
@@ -104,48 +151,7 @@
         hid[:, lanes] = (g * jax.nn.sigmoid(g) * u).astype(BF)
         return carry
 
-    for t in range(4):
-        lanes = slice(128 * t, 128 * (t + 1))
-        bt[lanes, :] = gout[:, lanes].astype(F32).T.astype(BF)
     lax.fori_loop(0, UN // 128, make_hidden, 0)
-    pl.semaphore_wait(barrier, ZN - 1 + 31)
-
-    def f_copy(k):
-        rows = pl.ds(hint(16 * k, 16), 16)
-        return remote(grot.at[rows, :], fin.at[z], f_s, f_r, i, 2 * k + c)
-
-    def f_start(j, carry):
-        k = (k_me + 4 + j) & 7
-
-        @pl.when(2 * k + c != z)
-        def _():
-            f_copy(k).start()
-
-        return carry
-
-    lax.fori_loop(0, 3, f_start, 0)
-
-    def b_copy(off):
-        peer = (xy + off) & 15
-        return remote(
-            bt.at[pl.ds(hint(COL * peer, COL), COL), :],
-            outs.at[pl.ds(hint(COL * z, COL), COL), pl.ds(hint(TOK * xy, TOK), TOK)],
-            b_s, b_r, 2 * peer + c, z,
-        )
-
-    def b_start(off, carry):
-        b_copy(off).start()
-        return carry
-
-    lax.fori_loop(1, XY, b_start, 0)
-    outs[pl.ds(hint(COL * z, COL), COL), pl.ds(hint(TOK * xy, TOK), TOK)] = bt[
-        pl.ds(hint(COL * xy, COL), COL), :
-    ]
-
-    @pl.when(active)
-    def _():
-        fin[z] = grot[pl.ds(hint(16 * k_me, 16), 16), :]
-
     load_table.wait()
     mine = pl.ds(hint(TOK * xy, TOK), TOK)
 
@@ -229,17 +235,11 @@
         taken(fin.at[pl.ds(0, ZN - 1)], f_r)
         rotate16(fin, fturn, 0, UN)
 
-        def fb_start(off, carry):
-            fb_copy((z + 7 + off) & 15).start()
+        def fb_start(t, carry):
+            fb_copy((z + far_first(t)) & 15).start()
             return carry
 
-        lax.fori_loop(1, 9, fb_start, 0)
-
-        def fb_start2(off, carry):
-            fb_copy((z + off) & 15).start()
-            return carry
-
-        lax.fori_loop(1, 8, fb_start2, 0)
+        lax.fori_loop(0, ZN - 1, fb_start, 0)
         fback[pl.ds(hint(16 * k_me, 16), 16), :] = fturn[z]
 
     def product(lanes, width):
@@ -276,13 +276,13 @@
         lanes = pl.ds(*CHUNKS[q])
         taken(other.at[:, :, lanes], e_r.at[q])
 
-        def add_send(off, carry):
-            j = (z + 8 + off) & 15
+        def add_send(t, carry):
+            j = (z + far_first(t)) & 15
             own[j, :, lanes] = (
                 part[j, pl.ds(hint(16 * c, 16), 16), lanes] + other[j, :, lanes].astype(F32)
             ).astype(BF)
 
-            @pl.when(j != z)
+            @pl.when(t < ZN - 1)
             def _():
                 g_copy(q, j).start()
 
@@ -336,7 +336,7 @@
         p, core, first, width, at = piece
 
         def z_start(off, carry):
-            z_copy(piece, (xy + off) & 15).start()
+            z_copy(piece, (xy + 7 * off) & 15).start()
             return carry
 
         lax.fori_loop(1, XY, z_start, 0)

time: 153 us -> 143 us (0.935)
  Pallas kernels: 147 us -> 138 us
    pallas_call x1, Pallas kernels: 147 us -> 138 us  [local(): pl.pallas_call(kernel, out_shape=(jax.ShapeDtypeStruct((TOK, UN), BF), ja...]
where the time goes in v3:
time: 143 us
  Pallas kernels  138 us (97%)
  other arithmetic  4.52 us (3%)
    pallas_call x1, Pallas kernels, local(): pl.pallas_call(kernel, out_shape=(jax.ShapeDtypeStruct((TOK, UN), BF), ja...  138 us

profile of v3, /device:TPU:1, one launch (start us, length us, event | category | flops | bytes accessed | tf_op | source)
XLA Modules:
  0.0 143.1 jit_solution(11587509240622926713)
XLA Ops:
  0.6 0.7 multiply_multiply_fusion
  1.3 0.0 copy-start.1
  1.3 0.0 copy-start.2
  1.3 137.8 %shard_map.103 = (bf16[128,1664]{1,0:T(8,128)(2,1)}, bf16[896,512]{1,0:T(8,128)(2,1)}) custom-call(bf16[128,1664]{1,0:T(8,128)(2,1)} %gate.1, bf16[128,1664]{1,0:T(8,128)(2,1)} %up.1, bf16[128,1664]{1,0:T(8,128)(2,1)} %grot.1, bf16[128,512]{1,0:T(8,128)(2,1)} %gout.1, bf16[1664,1664]{1,0:T(8,128)(2,1)} %constant.21.clone.table_hbm), custom_call_target="tpu_custom_call" | custom-call | tf_op jit(solution)/shard_map/pallas_call | solution.py:412
  139.2 0.0 copy-start
  139.2 0.0 copy-start.3
  139.2 0.0 copy-done.1
  139.2 0.0 copy-done.2
  139.2 2.5 %fusion.9 = (bf16[128,1664]{1,0:T(8,128)(2,1)}, bf16[128,1664]{1,0:T(8,128)(2,1)}) fusion(bf16[128,1664]{1,0:T(8,128)(2,1)S(1)} %copy-done.1, bf16[128,1664]{1,0:T(8,128)(2,1)} %get-tuple-element.5, bf16[128,1664]{1,0:T(8,128)(2,1)S(1)} %copy-done.2), kind=kLoop, calls=%fused_computation.14 | loop fusion | flops 3407872 | bytes 2129920 | tf_op jit(solution)/shard_map/convert_element_type | solution.py:455
  141.7 0.0 copy-done
  141.7 0.0 copy-done.3
  141.7 1.3 fusion
Async XLA Ops:
  1.3 137.9 %copy-start.1 = (bf16[128,1664]{1,0:T(8,128)(2,1)S(1)}, bf16[128,1664]{1,0:T(8,128)(2,1)}, u32[]{:S(2)}) copy-start(bf16[128,1664]{1,0:T(8,128)(2,1)} %gate.1) | copy-start | bytes 1277956
  1.3 137.9 %copy-start.2 = (bf16[128,1664]{1,0:T(8,128)(2,1)S(1)}, bf16[128,1664]{1,0:T(8,128)(2,1)}, u32[]{:S(2)}) copy-start(bf16[128,1664]{1,0:T(8,128)(2,1)} %up.1) | copy-start | bytes 1277956
  139.2 2.5 %copy-start = (bf16[896,512]{1,0:T(8,128)(2,1)S(1)}, bf16[896,512]{1,0:T(8,128)(2,1)}, u32[]{:S(2)}) copy-start(bf16[896,512]{1,0:T(8,128)(2,1)} %get-tuple-element.6) | copy-start | bytes 2752516
  139.2 2.5 %copy-start.3 = (bf16[832,512]{1,0:T(8,128)(2,1)S(1)}, bf16[832,512]{1,0:T(8,128)(2,1)}, u32[]{:S(2)}) copy-start(bf16[832,512]{1,0:T(8,128)(2,1)} %param.12) | copy-start | bytes 2555908

commit v4 on v3

--- a/solution.py
+++ b/solution.py
@@ -32,6 +32,7 @@
 
 
 CHUNKS = ((0, 896), (896, 384), (1280, 384))
+PASSES = ((0, 896), (896, 768))
 PIECES = (
     ((0, 0, 0, 896, 0), (1, 1, 768, 128, 0)),
     ((2, 1, 896, 384, 128),),
@@ -64,7 +65,7 @@
 def kernel(
     gate, up, grot, gout, table_hbm, gh_out, gw_out,
     acts, outs, part, send, other, own, got, turned, landed, hid, fin, fturn, fback,
-    bt, table, load_sem, ring_s, ring_r, f_s, f_r, fb_s, fb_r, b_s, b_r, e_s, e_r, g_s, g_r, z_s, z_r,
+    bt, table, load_sem, ring_s, ring_r, ring_rz, f_s, f_r, fb_s, fb_r, b_s, b_r, e_s, e_r, g_s, g_r, z_s, z_r,
 ):
     i = lax.axis_index("dp")
     z = lax.axis_index("tensor")
@@ -155,15 +156,22 @@
     load_table.wait()
     mine = pl.ds(hint(TOK * xy, TOK), TOK)
 
-    def turn_hidden(t, carry):
-        lanes = pl.ds(hint(t * 256, 256), 256)
+
+    def turn(lanes):
         acts[mine, lanes] = jnp.dot(hid[...], table[:, lanes], preferred_element_type=F32).astype(BF)
-        return carry
-
-    lax.fori_loop(0, UN // 256, turn_hidden, 0)
-    acts[mine, UN - 128 :] = jnp.dot(
-        hid[...], table[:, UN - 128 :], preferred_element_type=F32
-    ).astype(BF)
+
+    def turn_pass(q):
+        first, width = PASSES[q]
+
+        def turn_tile(t, carry):
+            turn(pl.ds(hint(first + t * 256, 128), 256))
+            return carry
+
+        lax.fori_loop(0, width // 256, turn_tile, 0)
+        if width % 256:
+            turn(pl.ds(first + width - 128, 128))
+
+    turn_pass(0)
 
     place = (4 * x + ((x + y) & 3), 4 * y + ((x + y) & 3), z)
 
@@ -179,50 +187,67 @@
 
     peers = [[ring_peer(r, (place[r] + hop) & 15) for hop in (1, 15)] for r in range(3)]
 
-    def ring_copy(r, d, s, u):
+    def ring_copy(q, r, d, s, u):
         blk = block_of(r, (place[r] + 16 - s if d == 0 else place[r] + s) & 15)
         if r < 2:
-            ref = acts.at[pl.ds(hint(TOK * blk + 64 * r + 32 * u, 32), 32), :]
+            ref = acts.at[pl.ds(hint(TOK * blk + 64 * r + 32 * u, 32), 32), pl.ds(*PASSES[q])]
+            sem = ring_r.at[q, r, d, s, u]
         else:
             ref = outs.at[pl.ds(hint(COL * blk + 16 * u, 16), 16), :]
-        return remote(ref, ref, ring_s.at[r], ring_r.at[r, d, s, u], *peers[r][d])
-
-    def ring_wait(r, d, s, u):
-        taken(acts.at[pl.ds(0, 32), :] if r < 2 else outs.at[pl.ds(0, 16), :], ring_r.at[r, d, s, u])
+            sem = ring_rz.at[d, s, u]
+        return remote(ref, ref, ring_s.at[r], sem, *peers[r][d])
+
+    def ring_wait(q, r, d, s, u):
+        if r < 2:
+            taken(acts.at[pl.ds(0, 32), pl.ds(*PASSES[q])], ring_r.at[q, r, d, s, u])
+        else:
+            taken(outs.at[pl.ds(0, 16), :], ring_rz.at[d, s, u])
+
+    def ring_step(q, rings, s):
+        for u in range(2):
+            for r in rings:
+                for d in range(2):
+                    ring_wait(q, r, d, s - 1, u)
+                    ring_copy(q, r, d, s, u).start()
+
+    def ring_last(q, rings):
+        for u in range(2):
+            for r in rings:
+                for d in range(2):
+                    ring_wait(q, r, d, 6, u)
+                    if u == d:
+                        ring_copy(q, r, d, 7, u).start()
+
+    def ring_end(q, rings):
+        for r in rings:
+            for d in range(2):
+                ring_wait(q, r, d, 7, d)
 
     for u in range(2):
         for r in range(2):
             for d in range(2):
-                ring_copy(r, d, 0, u).start()
+                ring_copy(0, r, d, 0, u).start()
 
     taken(outs.at[pl.ds(0, COL), pl.ds(0, TOK * (XY - 1))], b_r)
     for u in range(2):
         for d in range(2):
-            ring_copy(2, d, 0, u).start()
-
-    def ring_step(s, carry):
-        for u in range(2):
-            for r in (2, 0, 1):
-                for d in range(2):
-                    ring_wait(r, d, s - 1, u)
-                    ring_copy(r, d, s, u).start()
-        return carry
-
-    def ring_step_f(s, carry):
-        f_start(s + 2, 0)
-        return ring_step(s, carry)
-
-    lax.fori_loop(1, 6, ring_step_f, 0)
-    ring_step(6, 0)
+            ring_copy(0, 2, d, 0, u).start()
+    turn_pass(1)
+
+    def ring_steps(h, carry):
+        ring_step(0, (2, 0, 1), 2 * h + 1)
+        f_start(h + 3, 0)
+        ring_step(0, (2, 0, 1), 2 * h + 2)
+        return carry
+
+    lax.fori_loop(0, 3, ring_steps, 0)
+    ring_last(0, (2, 0, 1))
+    lax.fori_loop(6, 8, f_start, 0)
     for u in range(2):
-        for r in (2, 0, 1):
+        for r in range(2):
             for d in range(2):
-                ring_wait(r, d, 6, u)
-                if u == d:
-                    ring_copy(r, d, 7, u).start()
-    for r in (2, 0, 1):
-        for d in range(2):
-            ring_wait(r, d, 7, d)
+                ring_copy(1, r, d, 0, u).start()
+    ring_end(0, (2, 0, 1))
 
     def fb_copy(dest):
         return remote(
@@ -230,17 +255,21 @@
             fb_s, fb_r, i, dest,
         )
 
-    @pl.when(active)
-    def _():
-        taken(fin.at[pl.ds(0, ZN - 1)], f_r)
-        rotate16(fin, fturn, 0, UN)
-
-        def fb_start(t, carry):
-            fb_copy((z + far_first(t)) & 15).start()
-            return carry
-
-        lax.fori_loop(0, ZN - 1, fb_start, 0)
-        fback[pl.ds(hint(16 * k_me, 16), 16), :] = fturn[z]
+    def turn_back():
+        @pl.when(active)
+        def _():
+            taken(fin.at[pl.ds(0, ZN - 1)], f_r)
+            rotate16(fin, fturn, 0, UN)
+            fback[pl.ds(hint(16 * k_me, 16), 16), :] = fturn[z]
+
+    def send_back(first, last):
+        @pl.when(active)
+        def _():
+            def fb_start(t, carry):
+                fb_copy((z + far_first(t)) & 15).start()
+                return carry
+
+            lax.fori_loop(first, last, fb_start, 0)
 
     def product(lanes, width):
         tile = jnp.dot(outs[...], acts[:, lanes], preferred_element_type=F32)
@@ -272,9 +301,10 @@
             own.at[dest, :, lanes], got.at[z, :, lanes], g_s, g_r.at[q], i, dest
         )
 
-    def share(q):
+    def share(q, begin=0, end=ZN):
         lanes = pl.ds(*CHUNKS[q])
-        taken(other.at[:, :, lanes], e_r.at[q])
+        if begin == 0:
+            taken(other.at[:, :, lanes], e_r.at[q])
 
         def add_send(t, carry):
             j = (z + far_first(t)) & 15
@@ -288,14 +318,32 @@
 
             return carry
 
-        lax.fori_loop(0, ZN, add_send, 0)
-        got[z, :, lanes] = own[z, :, lanes]
-
+        lax.fori_loop(begin, end, add_send, 0)
+        if end == ZN:
+            got[z, :, lanes] = own[z, :, lanes]
+
+    ring_step(1, (0, 1), 1)
     product_chunk(0)
     swap(0).start()
+    ring_step(1, (0, 1), 2)
+    turn_back()
+    send_back(0, 4)
+    ring_step(1, (0, 1), 3)
+    share(0, 0, 5)
+    ring_step(1, (0, 1), 4)
+    share(0, 5, 9)
+    send_back(4, 7)
+    ring_step(1, (0, 1), 5)
+    share(0, 9, 13)
+    send_back(7, 10)
+    ring_step(1, (0, 1), 6)
+    share(0, 13, ZN)
+    send_back(10, 13)
+    ring_last(1, (0, 1))
+    send_back(13, 15)
+    ring_end(1, (0, 1))
     product_chunk(1)
     swap(1).start()
-    share(0)
     product_chunk(2)
     swap(2).start()
     share(1)
@@ -433,7 +481,7 @@
             pltpu.VMEM((TOK, UN), BF),
             pltpu.VMEM((512, TOK), BF),
             pltpu.VMEM((UN, UN), BF),
-            dma(()), dma((3,)), dma((3, 2, 8, 2)),
+            dma(()), dma((3,)), dma((2, 2, 2, 8, 2)), dma((2, 8, 2)),
             dma(()), dma(()), dma(()), dma(()),
             dma(()), dma(()), dma(()), dma((3,)),
             dma(()), dma((3,)), dma((4,)), dma((4,)),

time: 143 us -> 146 us (1.021)
  Pallas kernels: 138 us -> 141 us
    pallas_call x1, Pallas kernels: 138 us -> 141 us  [local(): pl.pallas_call(kernel, out_shape=(jax.ShapeDtypeStruct((TOK, UN), BF), ja...]
where the time goes in v4:
time: 146 us
  Pallas kernels  141 us (97%)
  other arithmetic  4.52 us (3%)
    pallas_call x1, Pallas kernels, local(): pl.pallas_call(kernel, out_shape=(jax.ShapeDtypeStruct((TOK, UN), BF), ja...  141 us

profile of v4, /device:TPU:1, one launch (start us, length us, event | category | flops | bytes accessed | tf_op | source)
XLA Modules:
  0.0 146.1 jit_solution(6463176888605313068)
XLA Ops:
  0.6 0.7 multiply_multiply_fusion
  1.3 0.0 copy-start.1
  1.3 0.0 copy-start.2
  1.3 140.9 %shard_map.103 = (bf16[128,1664]{1,0:T(8,128)(2,1)}, bf16[896,512]{1,0:T(8,128)(2,1)}) custom-call(bf16[128,1664]{1,0:T(8,128)(2,1)} %gate.1, bf16[128,1664]{1,0:T(8,128)(2,1)} %up.1, bf16[128,1664]{1,0:T(8,128)(2,1)} %grot.1, bf16[128,512]{1,0:T(8,128)(2,1)} %gout.1, bf16[1664,1664]{1,0:T(8,128)(2,1)} %constant.21.clone.table_hbm), custom_call_target="tpu_custom_call" | custom-call | tf_op jit(solution)/shard_map/pallas_call | solution.py:460
  142.2 0.0 copy-start
  142.2 0.0 copy-start.3
  142.3 0.0 copy-done.1
  142.3 0.0 copy-done.2
  142.3 2.5 %fusion.9 = (bf16[128,1664]{1,0:T(8,128)(2,1)}, bf16[128,1664]{1,0:T(8,128)(2,1)}) fusion(bf16[128,1664]{1,0:T(8,128)(2,1)S(1)} %copy-done.1, bf16[128,1664]{1,0:T(8,128)(2,1)} %get-tuple-element.5, bf16[128,1664]{1,0:T(8,128)(2,1)S(1)} %copy-done.2), kind=kLoop, calls=%fused_computation.14 | loop fusion | flops 3407872 | bytes 2129920 | tf_op jit(solution)/shard_map/convert_element_type | solution.py:503
  144.8 0.0 copy-done
  144.8 0.0 copy-done.3
  144.8 1.3 fusion
Async XLA Ops:
  1.3 140.9 %copy-start.1 = (bf16[128,1664]{1,0:T(8,128)(2,1)S(1)}, bf16[128,1664]{1,0:T(8,128)(2,1)}, u32[]{:S(2)}) copy-start(bf16[128,1664]{1,0:T(8,128)(2,1)} %gate.1) | copy-start | bytes 1277956
  1.3 140.9 %copy-start.2 = (bf16[128,1664]{1,0:T(8,128)(2,1)S(1)}, bf16[128,1664]{1,0:T(8,128)(2,1)}, u32[]{:S(2)}) copy-start(bf16[128,1664]{1,0:T(8,128)(2,1)} %up.1) | copy-start | bytes 1277956
  142.2 2.5 %copy-start = (bf16[896,512]{1,0:T(8,128)(2,1)S(1)}, bf16[896,512]{1,0:T(8,128)(2,1)}, u32[]{:S(2)}) copy-start(bf16[896,512]{1,0:T(8,128)(2,1)} %get-tuple-element.6) | copy-start | bytes 2752516
  142.2 2.5 %copy-start.3 = (bf16[832,512]{1,0:T(8,128)(2,1)S(1)}, bf16[832,512]{1,0:T(8,128)(2,1)}, u32[]{:S(2)}) copy-start(bf16[832,512]{1,0:T(8,128)(2,1)} %param.12) | copy-start | bytes 2555908

commit v5 on v3

--- a/solution.py
+++ b/solution.py
@@ -73,6 +73,7 @@
     x, y = xy >> 2, xy & 3
     k_me = z >> 1
     active = (z & 1) == c
+    sign = 1 - 2 * c
 
     def remote(src, dst, ssem, rsem, dp, zz):
         return pltpu.make_async_remote_copy(
@@ -102,26 +103,27 @@
     lax.fori_loop(1, ZN, hail_z, 0)
     lax.fori_loop(1, 32, hail_xy, 0)
 
+    pl.semaphore_wait(barrier, ZN - 1 + 31)
+
+    def f_copy(k):
+        rows = pl.ds(hint(16 * k, 16), 16)
+        return remote(grot.at[rows, :], fin.at[z], f_s, f_r, i, 2 * k + c)
+
+    def f_start(j, carry):
+        half = (j + 1) >> 1
+        k = (k_me + 4 + sign * half * (1 - 2 * (j & 1))) & 7
+
+        @pl.when(2 * k + c != z)
+        def _():
+            f_copy(k).start()
+
+        return carry
+
+    lax.fori_loop(0, 4, f_start, 0)
+
     for t in range(4):
         lanes = slice(128 * t, 128 * (t + 1))
         bt[lanes, :] = gout[:, lanes].astype(F32).T.astype(BF)
-    pl.semaphore_wait(barrier, ZN - 1 + 31)
-
-    def f_copy(k):
-        rows = pl.ds(hint(16 * k, 16), 16)
-        return remote(grot.at[rows, :], fin.at[z], f_s, f_r, i, 2 * k + c)
-
-    def f_start(j, carry):
-        half = (j + 1) >> 1
-        k = (k_me + 4 + half * (1 - 2 * (j & 1))) & 7
-
-        @pl.when(2 * k + c != z)
-        def _():
-            f_copy(k).start()
-
-        return carry
-
-    lax.fori_loop(0, 3, f_start, 0)
 
     def b_copy(off):
         peer = (xy + 7 * off) & 15
@@ -177,10 +179,10 @@
     def ring_peer(r, n):
         return (i, n) if r == 2 else (2 * block_of(r, n) + c, z)
 
-    peers = [[ring_peer(r, (place[r] + hop) & 15) for hop in (1, 15)] for r in range(3)]
+    peers = [[ring_peer(r, (place[r] + hop) & 15) for hop in (sign, -sign)] for r in range(3)]
 
     def ring_copy(r, d, s, u):
-        blk = block_of(r, (place[r] + 16 - s if d == 0 else place[r] + s) & 15)
+        blk = block_of(r, (place[r] - (1 - 2 * d) * sign * s) & 15)
         if r < 2:
             ref = acts.at[pl.ds(hint(TOK * blk + 64 * r + 32 * u, 32), 32), :]
         else:
@@ -209,38 +211,44 @@
         return carry
 
     def ring_step_f(s, carry):
-        f_start(s + 2, 0)
+        f_start(s + 3, 0)
         return ring_step(s, carry)
 
-    lax.fori_loop(1, 6, ring_step_f, 0)
-    ring_step(6, 0)
+    def fb_copy(dest):
+        return remote(
+            fturn.at[dest], fback.at[pl.ds(hint(16 * k_me, 16), 16), :],
+            fb_s, fb_r, i, dest,
+        )
+
+    def turn_back():
+        @pl.when(active)
+        def _():
+            taken(fin.at[pl.ds(0, ZN - 1)], f_r)
+            rotate16(fin, fturn, 0, UN)
+            fback[pl.ds(hint(16 * k_me, 16), 16), :] = fturn[z]
+
+    def send_back(first, last):
+        @pl.when(active)
+        def _():
+            def fb_start(t, carry):
+                fb_copy((z + sign * far_first(t)) & 15).start()
+                return carry
+
+            lax.fori_loop(first, last, fb_start, 0)
+
+    lax.fori_loop(1, 5, ring_step_f, 0)
+    lax.fori_loop(5, 7, ring_step, 0)
+    turn_back()
     for u in range(2):
         for r in (2, 0, 1):
             for d in range(2):
                 ring_wait(r, d, 6, u)
                 if u == d:
                     ring_copy(r, d, 7, u).start()
+    send_back(0, 4)
     for r in (2, 0, 1):
         for d in range(2):
             ring_wait(r, d, 7, d)
-
-    def fb_copy(dest):
-        return remote(
-            fturn.at[dest], fback.at[pl.ds(hint(16 * k_me, 16), 16), :],
-            fb_s, fb_r, i, dest,
-        )
-
-    @pl.when(active)
-    def _():
-        taken(fin.at[pl.ds(0, ZN - 1)], f_r)
-        rotate16(fin, fturn, 0, UN)
-
-        def fb_start(t, carry):
-            fb_copy((z + far_first(t)) & 15).start()
-            return carry
-
-        lax.fori_loop(0, ZN - 1, fb_start, 0)
-        fback[pl.ds(hint(16 * k_me, 16), 16), :] = fturn[z]
 
     def product(lanes, width):
         tile = jnp.dot(outs[...], acts[:, lanes], preferred_element_type=F32)
@@ -277,7 +285,7 @@
         taken(other.at[:, :, lanes], e_r.at[q])
 
         def add_send(t, carry):
-            j = (z + far_first(t)) & 15
+            j = (z + sign * far_first(t)) & 15
             own[j, :, lanes] = (
                 part[j, pl.ds(hint(16 * c, 16), 16), lanes] + other[j, :, lanes].astype(F32)
             ).astype(BF)
@@ -293,12 +301,16 @@
 
     product_chunk(0)
     swap(0).start()
+    send_back(4, 7)
     product_chunk(1)
     swap(1).start()
-    share(0)
+    send_back(7, 10)
     product_chunk(2)
     swap(2).start()
+    share(0)
+    send_back(10, 12)
     share(1)
+    send_back(12, 15)
     share(2)
 
     @pl.when(active)

time: 143 us -> 147 us (1.028)
  Pallas kernels: 138 us -> 141 us
    pallas_call x1, Pallas kernels: 138 us -> 141 us  [local(): pl.pallas_call(kernel, out_shape=(jax.ShapeDtypeStruct((TOK, UN), BF), ja...]
where the time goes in v5:
time: 147 us; the launch traced here: 146 us
  Pallas kernels  141 us (96%)
  other arithmetic  4.52 us (3%)
    pallas_call x1, Pallas kernels, local(): pl.pallas_call(kernel, out_shape=(jax.ShapeDtypeStruct((TOK, UN), BF), ja...  141 us

profile of v5, /device:TPU:1, one launch (start us, length us, event | category | flops | bytes accessed | tf_op | source)
XLA Modules:
  0.0 146.4 jit_solution(2667297972355930660)
XLA Ops:
  0.6 0.7 multiply_multiply_fusion
  1.3 0.0 copy-start.1
  1.3 0.0 copy-start.2
  1.3 141.2 %shard_map.103 = (bf16[128,1664]{1,0:T(8,128)(2,1)}, bf16[896,512]{1,0:T(8,128)(2,1)}) custom-call(bf16[128,1664]{1,0:T(8,128)(2,1)} %gate.1, bf16[128,1664]{1,0:T(8,128)(2,1)} %up.1, bf16[128,1664]{1,0:T(8,128)(2,1)} %grot.1, bf16[128,512]{1,0:T(8,128)(2,1)} %gout.1, bf16[1664,1664]{1,0:T(8,128)(2,1)} %constant.21.clone.table_hbm), custom_call_target="tpu_custom_call" | custom-call | tf_op jit(solution)/shard_map/pallas_call | solution.py:424
  142.6 0.0 copy-start
  142.6 0.0 copy-start.3
  142.6 0.0 copy-done.1
  142.6 0.0 copy-done.2
  142.6 2.5 %fusion.9 = (bf16[128,1664]{1,0:T(8,128)(2,1)}, bf16[128,1664]{1,0:T(8,128)(2,1)}) fusion(bf16[128,1664]{1,0:T(8,128)(2,1)S(1)} %copy-done.1, bf16[128,1664]{1,0:T(8,128)(2,1)} %get-tuple-element.5, bf16[128,1664]{1,0:T(8,128)(2,1)S(1)} %copy-done.2), kind=kLoop, calls=%fused_computation.14 | loop fusion | flops 3407872 | bytes 2129920 | tf_op jit(solution)/shard_map/convert_element_type | solution.py:467
  145.1 0.0 copy-done
  145.1 0.0 copy-done.3
  145.1 1.3 fusion
Async XLA Ops:
  1.3 141.3 %copy-start.1 = (bf16[128,1664]{1,0:T(8,128)(2,1)S(1)}, bf16[128,1664]{1,0:T(8,128)(2,1)}, u32[]{:S(2)}) copy-start(bf16[128,1664]{1,0:T(8,128)(2,1)} %gate.1) | copy-start | bytes 1277956
  1.3 141.3 %copy-start.2 = (bf16[128,1664]{1,0:T(8,128)(2,1)S(1)}, bf16[128,1664]{1,0:T(8,128)(2,1)}, u32[]{:S(2)}) copy-start(bf16[128,1664]{1,0:T(8,128)(2,1)} %up.1) | copy-start | bytes 1277956
  142.6 2.5 %copy-start = (bf16[896,512]{1,0:T(8,128)(2,1)S(1)}, bf16[896,512]{1,0:T(8,128)(2,1)}, u32[]{:S(2)}) copy-start(bf16[896,512]{1,0:T(8,128)(2,1)} %get-tuple-element.6) | copy-start | bytes 2752516
  142.6 2.5 %copy-start.3 = (bf16[832,512]{1,0:T(8,128)(2,1)S(1)}, bf16[832,512]{1,0:T(8,128)(2,1)}, u32[]{:S(2)}) copy-start(bf16[832,512]{1,0:T(8,128)(2,1)} %param.12) | copy-start | bytes 2555908

commit v6 on v3

--- a/solution.py
+++ b/solution.py
@@ -64,7 +64,7 @@
 def kernel(
     gate, up, grot, gout, table_hbm, gh_out, gw_out,
     acts, outs, part, send, other, own, got, turned, landed, hid, fin, fturn, fback,
-    bt, table, load_sem, ring_s, ring_r, f_s, f_r, fb_s, fb_r, b_s, b_r, e_s, e_r, g_s, g_r, z_s, z_r,
+    bt, table, load_sem, a_s, a_r, ring_s, ring_r, f_s, f_r, fb_s, fb_r, b_s, b_r, e_s, e_r, g_s, g_r, z_s, z_r,
 ):
     i = lax.axis_index("dp")
     z = lax.axis_index("tensor")
@@ -165,64 +165,105 @@
         hid[...], table[:, UN - 128 :], preferred_element_type=F32
     ).astype(BF)
 
-    place = (4 * x + ((x + y) & 3), 4 * y + ((x + y) & 3), z)
-
-    def block_of(r, n):
-        if r == 2:
-            return n
-        major = n >> 2
-        minor = (n + 3 * major) & 3
-        return 4 * major + minor if r == 0 else 4 * minor + major
-
-    def ring_peer(r, n):
-        return (i, n) if r == 2 else (2 * block_of(r, n) + c, z)
-
-    peers = [[ring_peer(r, (place[r] + hop) & 15) for hop in (1, 15)] for r in range(3)]
-
-    def ring_copy(r, d, s, u):
-        blk = block_of(r, (place[r] + 16 - s if d == 0 else place[r] + s) & 15)
-        if r < 2:
-            ref = acts.at[pl.ds(hint(TOK * blk + 64 * r + 32 * u, 32), 32), :]
-        else:
-            ref = outs.at[pl.ds(hint(COL * blk + 16 * u, 16), 16), :]
-        return remote(ref, ref, ring_s.at[r], ring_r.at[r, d, s, u], *peers[r][d])
-
-    def ring_wait(r, d, s, u):
-        taken(acts.at[pl.ds(0, 32), :] if r < 2 else outs.at[pl.ds(0, 16), :], ring_r.at[r, d, s, u])
-
-    for u in range(2):
-        for r in range(2):
+    COLS = (0, -1, 1, 2)
+
+    def chip(h, p, q):
+        return 4 * (p & 3) + (q & 3) if h == 0 else 4 * (q & 3) + (p & 3)
+
+    def spot(h):
+        return (x, y) if h == 0 else (y, x)
+
+    def a_rows(h, blk, part):
+        if part is None:
+            return acts.at[pl.ds(hint(TOK * blk + 64 * h, 64), 64), :]
+        return acts.at[pl.ds(hint(TOK * blk + 64 * h + 32 * part, 32), 32), :]
+
+    def a_send(h, first_axis, blk, part, d, sem):
+        p, q = spot(h)
+        hop = 1 - 2 * d
+        peer = chip(h, p + hop, q) if first_axis else chip(h, p, q + hop)
+        ref = a_rows(h, blk, part)
+        remote(ref, ref, a_s.at[h], a_r.at[h, sem, d], 2 * peer + c, z).start()
+
+    def a_take(h, rows, d, sem):
+        taken(acts.at[pl.ds(0, rows), :], a_r.at[h, sem, d])
+
+    def first_near(h, d):
+        a_send(h, True, chip(h, *spot(h)), None, d, 0)
+
+    def first_far(h, d):
+        p, q = spot(h)
+        a_send(h, True, chip(h, p - 1 + 2 * d, q), d, d, 1)
+
+    def second_near(h, j, d):
+        p, q = spot(h)
+        a_send(h, False, chip(h, p + COLS[j], q), None, d, 2 + j)
+
+    def second_far(h, j, d):
+        p, q = spot(h)
+        a_send(h, False, chip(h, p + COLS[j], q - 1 + 2 * d), d, d, 6 + j)
+
+    both = [(h, d) for d in range(2) for h in range(2)]
+    for h, d in both:
+        first_near(h, d)
+    for h, d in both:
+        second_near(h, 0, d)
+
+    def ring_copy(d, s, u):
+        origin = (z + 16 - s if d == 0 else z + s) & 15
+        ref = outs.at[pl.ds(hint(COL * origin + 16 * u, 16), 16), :]
+        peer = (z + 1 if d == 0 else z + 15) & 15
+        return remote(ref, ref, ring_s, ring_r.at[d, s, u], i, peer)
+
+    def ring_wait(d, s, u):
+        taken(outs.at[pl.ds(0, 16), :], ring_r.at[d, s, u])
+
+    def ring_step(s):
+        for u in range(2):
             for d in range(2):
-                ring_copy(r, d, 0, u).start()
+                ring_wait(d, s - 1, u)
+                if s < 7 or u == d:
+                    ring_copy(d, s, u).start()
 
     taken(outs.at[pl.ds(0, COL), pl.ds(0, TOK * (XY - 1))], b_r)
     for u in range(2):
         for d in range(2):
-            ring_copy(2, d, 0, u).start()
-
-    def ring_step(s, carry):
-        for u in range(2):
-            for r in (2, 0, 1):
-                for d in range(2):
-                    ring_wait(r, d, s - 1, u)
-                    ring_copy(r, d, s, u).start()
-        return carry
-
-    def ring_step_f(s, carry):
-        f_start(s + 2, 0)
-        return ring_step(s, carry)
-
-    lax.fori_loop(1, 6, ring_step_f, 0)
-    ring_step(6, 0)
-    for u in range(2):
-        for r in (2, 0, 1):
-            for d in range(2):
-                ring_wait(r, d, 6, u)
-                if u == d:
-                    ring_copy(r, d, 7, u).start()
-    for r in (2, 0, 1):
-        for d in range(2):
-            ring_wait(r, d, 7, d)
+            ring_copy(d, 0, u).start()
+
+    f_start(3, 0)
+    ring_step(1)
+    for h, d in both:
+        a_take(h, 64, d, 0)
+        first_far(h, d)
+    for h, d in both:
+        second_near(h, 1, d)
+    f_start(4, 0)
+    ring_step(2)
+    for h, d in both:
+        a_take(h, 64, d, 2)
+        second_far(h, 0, d)
+    for h, d in both:
+        second_near(h, 2, d)
+    f_start(5, 0)
+    ring_step(3)
+    for h, d in both:
+        a_take(h, 32, d, 1)
+    for h, d in both:
+        second_near(h, 3, d)
+    f_start(6, 0)
+    ring_step(4)
+    for j in range(1, 4):
+        for h, d in both:
+            a_take(h, 64, d, 2 + j)
+            second_far(h, j, d)
+        if j == 1:
+            f_start(7, 0)
+        ring_step(4 + j)
+    for d in range(2):
+        ring_wait(d, 7, d)
+    for j in range(4):
+        for h, d in both:
+            a_take(h, 32, d, 6 + j)
 
     def fb_copy(dest):
         return remote(
@@ -376,9 +417,9 @@
     for piece in PIECES[2]:
         z_take(piece)
 
-    for r in range(2):
-        gone(acts.at[pl.ds(0, 64 * 15), :], ring_s.at[r])
-    gone(outs.at[pl.ds(0, COL * 15), :], ring_s.at[2])
+    for h in range(2):
+        gone(acts.at[pl.ds(0, 64 * 15), :], a_s.at[h])
+    gone(outs.at[pl.ds(0, COL * 15), :], ring_s)
     gone(outs.at[pl.ds(0, COL), pl.ds(0, TOK * (XY - 1))], b_s)
 
     @pl.when(active)
@@ -433,7 +474,7 @@
             pltpu.VMEM((TOK, UN), BF),
             pltpu.VMEM((512, TOK), BF),
             pltpu.VMEM((UN, UN), BF),
-            dma(()), dma((3,)), dma((3, 2, 8, 2)),
+            dma(()), dma((2,)), dma((2, 10, 2)), dma(()), dma((2, 8, 2)),
             dma(()), dma(()), dma(()), dma(()),
             dma(()), dma(()), dma(()), dma((3,)),
             dma(()), dma((3,)), dma((4,)), dma((4,)),

time: 143 us -> 139 us (0.972)
  Pallas kernels: 138 us -> 134 us
    pallas_call x1, Pallas kernels: 138 us -> 134 us  [local(): pl.pallas_call(kernel, out_shape=(jax.ShapeDtypeStruct((TOK, UN), BF), ja...]
where the time goes in v6:
time: 139 us
  Pallas kernels  134 us (96%)
  other arithmetic  4.52 us (3%)
    pallas_call x1, Pallas kernels, local(): pl.pallas_call(kernel, out_shape=(jax.ShapeDtypeStruct((TOK, UN), BF), ja...  134 us

profile of v6, /device:TPU:1, one launch (start us, length us, event | category | flops | bytes accessed | tf_op | source)
XLA Modules:
  0.0 139.3 jit_solution(1388932494108602468)
XLA Ops:
  0.6 0.7 multiply_multiply_fusion
  1.3 0.0 copy-start.1
  1.3 0.0 copy-start.2
  1.3 134.0 %shard_map.103 = (bf16[128,1664]{1,0:T(8,128)(2,1)}, bf16[896,512]{1,0:T(8,128)(2,1)}) custom-call(bf16[128,1664]{1,0:T(8,128)(2,1)} %gate.1, bf16[128,1664]{1,0:T(8,128)(2,1)} %up.1, bf16[128,1664]{1,0:T(8,128)(2,1)} %grot.1, bf16[128,512]{1,0:T(8,128)(2,1)} %gout.1, bf16[1664,1664]{1,0:T(8,128)(2,1)} %constant.21.clone.table_hbm), custom_call_target="tpu_custom_call" | custom-call | tf_op jit(solution)/shard_map/pallas_call | solution.py:453
  135.4 0.0 copy-start
  135.4 0.0 copy-start.3
  135.4 0.0 copy-done.1
  135.4 0.0 copy-done.2
  135.4 2.5 %fusion.9 = (bf16[128,1664]{1,0:T(8,128)(2,1)}, bf16[128,1664]{1,0:T(8,128)(2,1)}) fusion(bf16[128,1664]{1,0:T(8,128)(2,1)S(1)} %copy-done.1, bf16[128,1664]{1,0:T(8,128)(2,1)} %get-tuple-element.5, bf16[128,1664]{1,0:T(8,128)(2,1)S(1)} %copy-done.2), kind=kLoop, calls=%fused_computation.14 | loop fusion | flops 3407872 | bytes 2129920 | tf_op jit(solution)/shard_map/convert_element_type | solution.py:496
  137.9 0.0 copy-done
  137.9 0.0 copy-done.3
  137.9 1.3 fusion
Async XLA Ops:
  1.3 134.1 %copy-start.1 = (bf16[128,1664]{1,0:T(8,128)(2,1)S(1)}, bf16[128,1664]{1,0:T(8,128)(2,1)}, u32[]{:S(2)}) copy-start(bf16[128,1664]{1,0:T(8,128)(2,1)} %gate.1) | copy-start | bytes 1277956
  1.3 134.1 %copy-start.2 = (bf16[128,1664]{1,0:T(8,128)(2,1)S(1)}, bf16[128,1664]{1,0:T(8,128)(2,1)}, u32[]{:S(2)}) copy-start(bf16[128,1664]{1,0:T(8,128)(2,1)} %up.1) | copy-start | bytes 1277956
  135.4 2.5 %copy-start = (bf16[896,512]{1,0:T(8,128)(2,1)S(1)}, bf16[896,512]{1,0:T(8,128)(2,1)}, u32[]{:S(2)}) copy-start(bf16[896,512]{1,0:T(8,128)(2,1)} %get-tuple-element.6) | copy-start | bytes 2752516
  135.4 2.5 %copy-start.3 = (bf16[832,512]{1,0:T(8,128)(2,1)S(1)}, bf16[832,512]{1,0:T(8,128)(2,1)}, u32[]{:S(2)}) copy-start(bf16[832,512]{1,0:T(8,128)(2,1)} %param.12) | copy-start | bytes 2555908

commit v7 on v6

--- a/solution.py
+++ b/solution.py
@@ -24,18 +24,21 @@
     table = np.array([[1.0]])
     for _ in range(6):
         table = np.block([[table, table], [table, -table]])
-    return np.kron(table / 8.0, np.eye(NBLK)).astype(jnp.bfloat16)
+    table = np.kron(table / 8.0, np.eye(NBLK)).astype(jnp.bfloat16)
+    order = np.concatenate([np.arange(832 * c + a, 832 * c + b) for a, b in ROWS for c in range(2)])
+    return np.stack([table, table[:, order]])
 
 
 def hint(value, multiple):
     return pl.multiple_of(value, multiple)
 
 
-CHUNKS = ((0, 896), (896, 384), (1280, 384))
+CHUNKS = ((0, 768), (768, 512), (1280, 384))
+ROWS = ((0, 384), (384, 640), (640, 832))
 PIECES = (
-    ((0, 0, 0, 896, 0), (1, 1, 768, 128, 0)),
-    ((2, 1, 896, 384, 128),),
-    ((3, 1, 1280, 384, 512),),
+    ((0, 0, 0, 384, 0), (1, 1, 384, 384, 0)),
+    ((2, 0, 768, 256, 384), (3, 1, 1024, 256, 384)),
+    ((4, 0, 1280, 256, 640), (5, 1, 1408, 256, 640)),
 )
 
 
@@ -62,9 +65,9 @@
 
 
 def kernel(
-    gate, up, grot, gout, table_hbm, gh_out, gw_out,
+    gate, up, grot, gout, tables, gg, gu, gw_out,
     acts, outs, part, send, other, own, got, turned, landed, hid, fin, fturn, fback,
-    bt, table, load_sem, a_s, a_r, ring_s, ring_r, f_s, f_r, fb_s, fb_r, b_s, b_r, e_s, e_r, g_s, g_r, z_s, z_r,
+    bt, table, ordered, load_sem, load_sem2, a_s, a_r, ring_s, ring_r, f_s, f_r, fb_s, fb_r, b_s, b_r, e_s, e_r, g_s, g_r, z_s, z_r,
 ):
     i = lax.axis_index("dp")
     z = lax.axis_index("tensor")
@@ -80,7 +83,9 @@
             device_id=(dp, zz), device_id_type=MESH,
         )
 
-    load_table = pltpu.make_async_copy(table_hbm, table, load_sem)
+    load_table = pltpu.make_async_copy(tables.at[0], table, load_sem)
+    load_ordered = pltpu.make_async_copy(tables.at[1], ordered, load_sem2)
+    load_ordered.start()
     load_table.start()
 
     def taken(ref, sem):
@@ -101,27 +106,28 @@
 
     lax.fori_loop(1, ZN, hail_z, 0)
     lax.fori_loop(1, 32, hail_xy, 0)
+
+    pl.semaphore_wait(barrier, ZN - 1 + 31)
+
+    def f_copy(k):
+        rows = pl.ds(hint(16 * k, 16), 16)
+        return remote(grot.at[rows, :], fin.at[z], f_s, f_r, i, 2 * k + c)
+
+    def f_start(j, carry):
+        half = (j + 1) >> 1
+        k = (k_me + 4 + half * (1 - 2 * (j & 1))) & 7
+
+        @pl.when(2 * k + c != z)
+        def _():
+            f_copy(k).start()
+
+        return carry
+
+    lax.fori_loop(0, 3, f_start, 0)
 
     for t in range(4):
         lanes = slice(128 * t, 128 * (t + 1))
         bt[lanes, :] = gout[:, lanes].astype(F32).T.astype(BF)
-    pl.semaphore_wait(barrier, ZN - 1 + 31)
-
-    def f_copy(k):
-        rows = pl.ds(hint(16 * k, 16), 16)
-        return remote(grot.at[rows, :], fin.at[z], f_s, f_r, i, 2 * k + c)
-
-    def f_start(j, carry):
-        half = (j + 1) >> 1
-        k = (k_me + 4 + half * (1 - 2 * (j & 1))) & 7
-
-        @pl.when(2 * k + c != z)
-        def _():
-            f_copy(k).start()
-
-        return carry
-
-    lax.fori_loop(0, 3, f_start, 0)
 
     def b_copy(off):
         peer = (xy + 7 * off) & 15
@@ -152,17 +158,17 @@
         return carry
 
     lax.fori_loop(0, UN // 128, make_hidden, 0)
-    load_table.wait()
+    load_ordered.wait()
     mine = pl.ds(hint(TOK * xy, TOK), TOK)
 
     def turn_hidden(t, carry):
         lanes = pl.ds(hint(t * 256, 256), 256)
-        acts[mine, lanes] = jnp.dot(hid[...], table[:, lanes], preferred_element_type=F32).astype(BF)
+        acts[mine, lanes] = jnp.dot(hid[...], ordered[:, lanes], preferred_element_type=F32).astype(BF)
         return carry
 
     lax.fori_loop(0, UN // 256, turn_hidden, 0)
     acts[mine, UN - 128 :] = jnp.dot(
-        hid[...], table[:, UN - 128 :], preferred_element_type=F32
+        hid[...], ordered[:, UN - 128 :], preferred_element_type=F32
     ).astype(BF)
 
     COLS = (0, -1, 1, 2)
@@ -351,7 +357,14 @@
         taken(fback, fb_r)
 
     def finish(lanes):
-        gh_out[:, lanes] = jnp.dot(fback[...], table[:, lanes], preferred_element_type=F32).astype(BF)
+        gh = jnp.dot(fback[...], table[:, lanes], preferred_element_type=F32)
+        g = gate[:, lanes].astype(F32)
+        u = up[:, lanes].astype(F32)
+        sg = jax.nn.sigmoid(g)
+        gg[:, lanes] = (gh * u * sg * (1.0 + g * (1.0 - sg))).astype(BF)
+        gu[:, lanes] = (gh * g * sg).astype(BF)
+
+    load_table.wait()
 
     def finish_tile(t, carry):
         finish(pl.ds(hint(t * 256, 256), 256))
@@ -399,12 +412,20 @@
         def _():
             taken(landed.at[pl.ds(0, 496), pl.ds(at, width)], z_r.at[p])
 
-            def flip(t, carry):
-                lanes = pl.ds(hint(t * 128, 128), 128)
-                gw_out[lanes, :] = landed[:, lanes].astype(F32).T.astype(BF)
-                return carry
-
-            lax.fori_loop(at // 128, (at + width) // 128, flip, 0)
+            def flip(t):
+                return landed[:, at + 128 * t : at + 128 * (t + 1)].astype(F32).T.astype(BF)
+
+            if width == 256 and at == 640:
+                one, two = flip(0), flip(1)
+                if core == 0:
+                    gw_out[640:768, :] = one
+                    gw_out[768:832, :] = two[:64]
+                else:
+                    gw_out[640:704, :] = one[64:]
+                    gw_out[704:832, :] = two
+            else:
+                for t in range(width // 128):
+                    gw_out[at + 128 * t : at + 128 * (t + 1), :] = flip(t)
 
     for q in range(3):
         g_wait_chunk(q)
@@ -445,19 +466,38 @@
                 gone(turned.at[:, :, pl.ds(first, width)], z_s.at[p])
 
 
+def last(gg_in, gu_in, summed, latent, codes, bits, gg, gu, gw, sem):
+    moves = [pltpu.make_async_copy(src, dst, sem.at[n]) for n, (src, dst) in enumerate(((gg_in, gg), (gu_in, gu)))]
+    for move in moves:
+        move.start()
+    levels = jnp.left_shift(jnp.int32(1), bits[...] - 1) - 1
+    limit = codes[...].astype(F32) * levels.astype(F32) / 65536.0
+
+    def mask(t, carry):
+        rows = pl.ds(hint(t * 64, 64), 64)
+        inside = jnp.abs(latent[rows, :].astype(F32)) <= limit
+        gw[rows, :] = jnp.where(inside, summed[rows, :].astype(F32), 0.0).astype(BF)
+        return carry
+
+    lax.fori_loop(0, 13, mask, 0)
+    for move in moves:
+        move.wait()
+
+
 def local(gate_pre, up_pre, grad_rot, grad_out, latent_weight, clip_codes, bits):
-    table = jnp.asarray(local_table())
+    tables = jnp.asarray(local_table())
     vmem = pl.BlockSpec(memory_space=pltpu.VMEM)
     hbm = pl.BlockSpec(memory_space=pl.ANY)
     dma = pltpu.SemaphoreType.DMA
-    grad_hidden, summed = pl.pallas_call(
+    grad_gate, grad_up, summed = pl.pallas_call(
         kernel,
         out_shape=(
             jax.ShapeDtypeStruct((TOK, UN), BF),
-            jax.ShapeDtypeStruct((HALF, 512), BF),
+            jax.ShapeDtypeStruct((TOK, UN), BF),
+            jax.ShapeDtypeStruct((832, 512), BF),
         ),
         in_specs=[vmem] * 4 + [hbm],
-        out_specs=(vmem, vmem),
+        out_specs=(vmem, vmem, vmem),
         scratch_shapes=[
             pltpu.VMEM((XY * TOK, UN), BF),
             pltpu.VMEM((512, XY * TOK), BF),
@@ -474,27 +514,27 @@
             pltpu.VMEM((TOK, UN), BF),
             pltpu.VMEM((512, TOK), BF),
             pltpu.VMEM((UN, UN), BF),
-            dma(()), dma((2,)), dma((2, 10, 2)), dma(()), dma((2, 8, 2)),
+            pltpu.VMEM((UN, UN), BF),
+            dma(()), dma(()), dma((2,)), dma((2, 10, 2)), dma(()), dma((2, 8, 2)),
             dma(()), dma(()), dma(()), dma(()),
             dma(()), dma(()), dma(()), dma((3,)),
-            dma(()), dma((3,)), dma((4,)), dma((4,)),
+            dma(()), dma((3,)), dma((6,)), dma((6,)),
         ],
         compiler_params=pltpu.CompilerParams(
             collective_id=0, has_side_effects=True, vmem_limit_bytes=56 * 1024 * 1024
         ),
-    )(gate_pre, up_pre, grad_rot, grad_out, table)
-    core = lax.axis_index("dp") & 1
-    rows = jnp.where(core == 1, summed[HALF - 832 :], summed[:832])
-    levels = jnp.left_shift(jnp.int32(1), bits - 1) - 1
-    clip_bound = clip_codes.astype(F32) * levels.astype(F32) / 65536.0
-    inside = jnp.abs(latent_weight.astype(F32)) <= clip_bound[None, :]
-    grad_weight = jnp.where(inside, rows, jnp.zeros((), BF))
-    gate_vals, up_vals = gate_pre.astype(F32), up_pre.astype(F32)
-    gh = grad_hidden.astype(F32)
-    sg = jax.nn.sigmoid(gate_vals)
-    grad_gate = (gh * up_vals * sg * (1.0 + gate_vals * (1.0 - sg))).astype(BF)
-    grad_up = (gh * gate_vals * sg).astype(BF)
-    return grad_gate, grad_up, grad_weight
+    )(gate_pre, up_pre, grad_rot, grad_out, tables)
+    return pl.pallas_call(
+        last,
+        out_shape=(
+            jax.ShapeDtypeStruct((TOK, UN), BF),
+            jax.ShapeDtypeStruct((TOK, UN), BF),
+            jax.ShapeDtypeStruct((832, 512), BF),
+        ),
+        in_specs=[hbm] * 2 + [vmem] * 4,
+        out_specs=(hbm, hbm, vmem),
+        scratch_shapes=[dma((2,))],
+    )(grad_gate, grad_up, summed, latent_weight, clip_codes[None, :], bits[None, :])
 
 
 def solution(mesh):

time: 139 us -> 164 us (1.18)
  Pallas kernels: 134 us -> 164 us
  other arithmetic: 4.52 us -> 0 us
    pallas_call x0 -> x1, Pallas kernels: none -> 29.2 us  [local(): pl.pallas_call(last, out_shape=(jax.ShapeDtypeStruct((TOK, UN), BF), jax....]
    convert_element_type x1 -> x0, other arithmetic: 2.48 us -> none  [local(): grad_up = (gh * gate_vals * sg).astype(BF)]
where the time goes in v7:
time: 164 us
  Pallas kernels  164 us (100%)
    pallas_call x1, Pallas kernels, local(): pl.pallas_call(kernel, out_shape=(jax.ShapeDtypeStruct((TOK, UN), BF), ja...  134 us
    pallas_call x1, Pallas kernels, local(): pl.pallas_call(last, out_shape=(jax.ShapeDtypeStruct((TOK, UN), BF), jax....  29.2 us

profile of v7, /device:TPU:1, one launch (start us, length us, event | category | flops | bytes accessed | tf_op | source)
XLA Modules:
  0.0 164.2 jit_solution(5100062352919014409)
XLA Ops:
  0.6 134.3 %shard_map.103 = (bf16[128,1664]{1,0:T(8,128)(2,1)}, bf16[128,1664]{1,0:T(8,128)(2,1)}, bf16[832,512]{1,0:T(8,128)(2,1)}) custom-call(bf16[128,1664]{1,0:T(8,128)(2,1)} %gate.1, bf16[128,1664]{1,0:T(8,128)(2,1)} %up.1, bf16[128,1664]{1,0:T(8,128)(2,1)} %grot.1, bf16[128,512]{1,0:T(8,128)(2,1)} %gout.1, bf16[2,1664,1664]{2,1,0:T(8,128)(2,1)} %constant.2.clone.tables), custom_call_target="tpu_custom_call" | custom-call | tf_op jit(solution)/shard_map/pallas_call | solution.py:492
  134.9 29.2 %shard_map.104 = (bf16[128,1664]{1,0:T(8,128)(2,1)}, bf16[128,1664]{1,0:T(8,128)(2,1)}, bf16[832,512]{1,0:T(8,128)(2,1)}) custom-call(bf16[128,1664]{1,0:T(8,128)(2,1)} %get-tuple-element.6.gg_in, bf16[128,1664]{1,0:T(8,128)(2,1)} %get-tuple-element.7.gu_in, bf16[832,512]{1,0:T(8,128)(2,1)} %get-tuple-element.8.summed, bf16[832,512]{1,0:T(8,128)(2,1)} %latent.1, ...), custom_call_target="tpu_custom_call" | custom-call | tf_op jit(solution)/shard_map/pallas_call | solution.py:527

commit v8 on v7

--- a/solution.py
+++ b/solution.py
@@ -83,10 +83,15 @@
             device_id=(dp, zz), device_id_type=MESH,
         )
 
-    load_table = pltpu.make_async_copy(tables.at[0], table, load_sem)
-    load_ordered = pltpu.make_async_copy(tables.at[1], ordered, load_sem2)
-    load_ordered.start()
-    load_table.start()
+    def load(n, dst, sem):
+        def load_rows(t, carry):
+            rows = pl.ds(hint(t * 128, 128), 128)
+            pltpu.make_async_copy(tables.at[n, rows, :], dst.at[rows, :], sem).start()
+            return carry
+
+        lax.fori_loop(0, UN // 128, load_rows, 0)
+
+    load(1, ordered, load_sem2)
 
     def taken(ref, sem):
         remote(ref, ref, load_sem, sem, i, z ^ 1).wait_recv()
@@ -158,7 +163,7 @@
         return carry
 
     lax.fori_loop(0, UN // 128, make_hidden, 0)
-    load_ordered.wait()
+    pltpu.make_async_copy(tables.at[1], ordered, load_sem2).wait()
     mine = pl.ds(hint(TOK * xy, TOK), TOK)
 
     def turn_hidden(t, carry):
@@ -214,6 +219,8 @@
         first_near(h, d)
     for h, d in both:
         second_near(h, 0, d)
+
+    load(0, table, load_sem)
 
     def ring_copy(d, s, u):
         origin = (z + 16 - s if d == 0 else z + s) & 15
@@ -265,29 +272,29 @@
         if j == 1:
             f_start(7, 0)
         ring_step(4 + j)
+    def fb_copy(dest):
+        return remote(
+            fturn.at[dest], fback.at[pl.ds(hint(16 * k_me, 16), 16), :],
+            fb_s, fb_r, i, dest,
+        )
+
+    @pl.when(active)
+    def _():
+        taken(fin.at[pl.ds(0, ZN - 1)], f_r)
+        rotate16(fin, fturn, 0, UN)
+
+        def fb_start(t, carry):
+            fb_copy((z + far_first(t)) & 15).start()
+            return carry
+
+        lax.fori_loop(0, ZN - 1, fb_start, 0)
+        fback[pl.ds(hint(16 * k_me, 16), 16), :] = fturn[z]
+
     for d in range(2):
         ring_wait(d, 7, d)
     for j in range(4):
         for h, d in both:
             a_take(h, 32, d, 6 + j)
-
-    def fb_copy(dest):
-        return remote(
-            fturn.at[dest], fback.at[pl.ds(hint(16 * k_me, 16), 16), :],
-            fb_s, fb_r, i, dest,
-        )
-
-    @pl.when(active)
-    def _():
-        taken(fin.at[pl.ds(0, ZN - 1)], f_r)
-        rotate16(fin, fturn, 0, UN)
-
-        def fb_start(t, carry):
-            fb_copy((z + far_first(t)) & 15).start()
-            return carry
-
-        lax.fori_loop(0, ZN - 1, fb_start, 0)
-        fback[pl.ds(hint(16 * k_me, 16), 16), :] = fturn[z]
 
     def product(lanes, width):
         tile = jnp.dot(outs[...], acts[:, lanes], preferred_element_type=F32)
@@ -364,7 +371,7 @@
         gg[:, lanes] = (gh * u * sg * (1.0 + g * (1.0 - sg))).astype(BF)
         gu[:, lanes] = (gh * g * sg).astype(BF)
 
-    load_table.wait()
+    pltpu.make_async_copy(tables.at[0], table, load_sem).wait()
 
     def finish_tile(t, carry):
         finish(pl.ds(hint(t * 256, 256), 256))
@@ -466,10 +473,7 @@
                 gone(turned.at[:, :, pl.ds(first, width)], z_s.at[p])
 
 
-def last(gg_in, gu_in, summed, latent, codes, bits, gg, gu, gw, sem):
-    moves = [pltpu.make_async_copy(src, dst, sem.at[n]) for n, (src, dst) in enumerate(((gg_in, gg), (gu_in, gu)))]
-    for move in moves:
-        move.start()
+def last(gg_in, gu_in, summed, latent, codes, bits, gg, gu, gw):
     levels = jnp.left_shift(jnp.int32(1), bits[...] - 1) - 1
     limit = codes[...].astype(F32) * levels.astype(F32) / 65536.0
 
@@ -480,8 +484,8 @@
         return carry
 
     lax.fori_loop(0, 13, mask, 0)
-    for move in moves:
-        move.wait()
+    gg[...] = gg_in[...]
+    gu[...] = gu_in[...]
 
 
 def local(gate_pre, up_pre, grad_rot, grad_out, latent_weight, clip_codes, bits):
@@ -531,9 +535,8 @@
             jax.ShapeDtypeStruct((TOK, UN), BF),
             jax.ShapeDtypeStruct((832, 512), BF),
         ),
-        in_specs=[hbm] * 2 + [vmem] * 4,
-        out_specs=(hbm, hbm, vmem),
-        scratch_shapes=[dma((2,))],
+        in_specs=[vmem] * 6,
+        out_specs=(vmem, vmem, vmem),
     )(grad_gate, grad_up, summed, latent_weight, clip_codes[None, :], bits[None, :])
 
 

time: 164 us -> 135 us (0.82)
  Pallas kernels: 164 us -> 134 us
    pallas_call x1, Pallas kernels: 29.2 us -> 3.25 us  [local(): pl.pallas_call(last, out_shape=(jax.ShapeDtypeStruct((TOK, UN), BF), jax....]
    pallas_call x1, Pallas kernels: 134 us -> 131 us  [local(): pl.pallas_call(kernel, out_shape=(jax.ShapeDtypeStruct((TOK, UN), BF), ja...]
where the time goes in v8:
time: 135 us
  Pallas kernels  134 us (99%)
    pallas_call x1, Pallas kernels, local(): pl.pallas_call(kernel, out_shape=(jax.ShapeDtypeStruct((TOK, UN), BF), ja...  131 us
    pallas_call x1, Pallas kernels, local(): pl.pallas_call(last, out_shape=(jax.ShapeDtypeStruct((TOK, UN), BF), jax....  3.25 us

profile of v8, /device:TPU:1, one launch (start us, length us, event | category | flops | bytes accessed | tf_op | source)
XLA Modules:
  0.0 134.5 jit_solution(18427104047544715874)
XLA Ops:
  0.6 130.7 %shard_map.103 = (bf16[128,1664]{1,0:T(8,128)(2,1)}, bf16[128,1664]{1,0:T(8,128)(2,1)}, bf16[832,512]{1,0:T(8,128)(2,1)}) custom-call(bf16[128,1664]{1,0:T(8,128)(2,1)} %gate.1, bf16[128,1664]{1,0:T(8,128)(2,1)} %up.1, bf16[128,1664]{1,0:T(8,128)(2,1)} %grot.1, bf16[128,512]{1,0:T(8,128)(2,1)} %gout.1, bf16[2,1664,1664]{2,1,0:T(8,128)(2,1)} %constant.2.clone.tables), custom_call_target="tpu_custom_call" | custom-call | tf_op jit(solution)/shard_map/pallas_call | solution.py:496
  131.3 3.3 %shard_map.104 = (bf16[128,1664]{1,0:T(8,128)(2,1)}, bf16[128,1664]{1,0:T(8,128)(2,1)}, bf16[832,512]{1,0:T(8,128)(2,1)}) custom-call(bf16[128,1664]{1,0:T(8,128)(2,1)} %get-tuple-element.6.gg_in, bf16[128,1664]{1,0:T(8,128)(2,1)} %get-tuple-element.7.gu_in, bf16[832,512]{1,0:T(8,128)(2,1)} %get-tuple-element.8.summed, bf16[832,512]{1,0:T(8,128)(2,1)} %latent.1, ...), custom_call_target="tpu_custom_call" | custom-call | tf_op jit(solution)/shard_map/pallas_call | solution.py:531

commit v9 on v8

--- a/solution.py
+++ b/solution.py
@@ -214,12 +214,6 @@
         p, q = spot(h)
         a_send(h, False, chip(h, p + COLS[j], q - 1 + 2 * d), d, d, 6 + j)
 
-    both = [(h, d) for d in range(2) for h in range(2)]
-    for h, d in both:
-        first_near(h, d)
-    for h, d in both:
-        second_near(h, 0, d)
-
     load(0, table, load_sem)
 
     def ring_copy(d, s, u):
@@ -242,6 +236,12 @@
     for u in range(2):
         for d in range(2):
             ring_copy(d, 0, u).start()
+
+    both = [(h, d) for d in range(2) for h in range(2)]
+    for h, d in both:
+        first_near(h, d)
+    for h, d in both:
+        second_near(h, 0, d)
 
     f_start(3, 0)
     ring_step(1)
@@ -278,17 +278,22 @@
             fb_s, fb_r, i, dest,
         )
 
+    def send_back(first, last_one):
+        @pl.when(active)
+        def _():
+            def fb_start(t, carry):
+                fb_copy((z + far_first(t)) & 15).start()
+                return carry
+
+            lax.fori_loop(first, last_one, fb_start, 0)
+
     @pl.when(active)
     def _():
         taken(fin.at[pl.ds(0, ZN - 1)], f_r)
         rotate16(fin, fturn, 0, UN)
-
-        def fb_start(t, carry):
-            fb_copy((z + far_first(t)) & 15).start()
-            return carry
-
-        lax.fori_loop(0, ZN - 1, fb_start, 0)
         fback[pl.ds(hint(16 * k_me, 16), 16), :] = fturn[z]
+
+    send_back(0, 5)
 
     for d in range(2):
         ring_wait(d, 7, d)
@@ -347,6 +352,7 @@
 
     product_chunk(0)
     swap(0).start()
+    send_back(5, ZN - 1)
     product_chunk(1)
     swap(1).start()
     share(0)

time: 135 us -> 137 us (1.015)
  Pallas kernels: 134 us -> 136 us
    pallas_call x1, Pallas kernels: 131 us -> 133 us  [local(): pl.pallas_call(kernel, out_shape=(jax.ShapeDtypeStruct((TOK, UN), BF), ja...]
where the time goes in v9:
time: 137 us
  Pallas kernels  136 us (99%)
    pallas_call x1, Pallas kernels, local(): pl.pallas_call(kernel, out_shape=(jax.ShapeDtypeStruct((TOK, UN), BF), ja...  133 us
    pallas_call x1, Pallas kernels, local(): pl.pallas_call(last, out_shape=(jax.ShapeDtypeStruct((TOK, UN), BF), jax....  3.25 us

profile of v9, /device:TPU:1, one launch (start us, length us, event | category | flops | bytes accessed | tf_op | source)
XLA Modules:
  0.0 136.8 jit_solution(6644763496266466713)
XLA Ops:
  0.6 132.9 %shard_map.103 = (bf16[128,1664]{1,0:T(8,128)(2,1)}, bf16[128,1664]{1,0:T(8,128)(2,1)}, bf16[832,512]{1,0:T(8,128)(2,1)}) custom-call(bf16[128,1664]{1,0:T(8,128)(2,1)} %gate.1, bf16[128,1664]{1,0:T(8,128)(2,1)} %up.1, bf16[128,1664]{1,0:T(8,128)(2,1)} %grot.1, bf16[128,512]{1,0:T(8,128)(2,1)} %gout.1, bf16[2,1664,1664]{2,1,0:T(8,128)(2,1)} %constant.2.clone.tables), custom_call_target="tpu_custom_call" | custom-call | tf_op jit(solution)/shard_map/pallas_call | solution.py:502
  133.6 3.3 %shard_map.104 = (bf16[128,1664]{1,0:T(8,128)(2,1)}, bf16[128,1664]{1,0:T(8,128)(2,1)}, bf16[832,512]{1,0:T(8,128)(2,1)}) custom-call(bf16[128,1664]{1,0:T(8,128)(2,1)} %get-tuple-element.6.gg_in, bf16[128,1664]{1,0:T(8,128)(2,1)} %get-tuple-element.7.gu_in, bf16[832,512]{1,0:T(8,128)(2,1)} %get-tuple-element.8.summed, bf16[832,512]{1,0:T(8,128)(2,1)} %latent.1, ...), custom_call_target="tpu_custom_call" | custom-call | tf_op jit(solution)/shard_map/pallas_call | solution.py:537

commit v10 on v8

--- a/solution.py
+++ b/solution.py
@@ -128,7 +128,7 @@
 
         return carry
 
-    lax.fori_loop(0, 3, f_start, 0)
+    lax.fori_loop(0, 4, f_start, 0)
 
     for t in range(4):
         lanes = slice(128 * t, 128 * (t + 1))
@@ -243,35 +243,34 @@
         for d in range(2):
             ring_copy(d, 0, u).start()
 
-    f_start(3, 0)
+    f_start(4, 0)
     ring_step(1)
     for h, d in both:
         a_take(h, 64, d, 0)
         first_far(h, d)
     for h, d in both:
         second_near(h, 1, d)
-    f_start(4, 0)
+    f_start(5, 0)
     ring_step(2)
     for h, d in both:
         a_take(h, 64, d, 2)
         second_far(h, 0, d)
     for h, d in both:
         second_near(h, 2, d)
-    f_start(5, 0)
+    f_start(6, 0)
     ring_step(3)
     for h, d in both:
         a_take(h, 32, d, 1)
     for h, d in both:
         second_near(h, 3, d)
-    f_start(6, 0)
+    f_start(7, 0)
     ring_step(4)
-    for j in range(1, 4):
+    for j in range(1, 3):
         for h, d in both:
             a_take(h, 64, d, 2 + j)
             second_far(h, j, d)
-        if j == 1:
-            f_start(7, 0)
         ring_step(4 + j)
+
     def fb_copy(dest):
         return remote(
             fturn.at[dest], fback.at[pl.ds(hint(16 * k_me, 16), 16), :],
@@ -290,6 +289,10 @@
         lax.fori_loop(0, ZN - 1, fb_start, 0)
         fback[pl.ds(hint(16 * k_me, 16), 16), :] = fturn[z]
 
+    for h, d in both:
+        a_take(h, 64, d, 5)
+        second_far(h, 3, d)
+    ring_step(7)
     for d in range(2):
         ring_wait(d, 7, d)
     for j in range(4):

time: 135 us -> 138 us (1.022)
  Pallas kernels: 134 us -> 137 us
    pallas_call x1, Pallas kernels: 131 us -> 134 us  [local(): pl.pallas_call(kernel, out_shape=(jax.ShapeDtypeStruct((TOK, UN), BF), ja...]
where the time goes in v10:
time: 138 us
  Pallas kernels  137 us (99%)
    pallas_call x1, Pallas kernels, local(): pl.pallas_call(kernel, out_shape=(jax.ShapeDtypeStruct((TOK, UN), BF), ja...  134 us
    pallas_call x1, Pallas kernels, local(): pl.pallas_call(last, out_shape=(jax.ShapeDtypeStruct((TOK, UN), BF), jax....  3.25 us

profile of v10, /device:TPU:1, one launch (start us, length us, event | category | flops | bytes accessed | tf_op | source)
XLA Modules:
  0.0 138.0 jit_solution(10783750922607440609)
XLA Ops:
  0.6 134.1 %shard_map.103 = (bf16[128,1664]{1,0:T(8,128)(2,1)}, bf16[128,1664]{1,0:T(8,128)(2,1)}, bf16[832,512]{1,0:T(8,128)(2,1)}) custom-call(bf16[128,1664]{1,0:T(8,128)(2,1)} %gate.1, bf16[128,1664]{1,0:T(8,128)(2,1)} %up.1, bf16[128,1664]{1,0:T(8,128)(2,1)} %grot.1, bf16[128,512]{1,0:T(8,128)(2,1)} %gout.1, bf16[2,1664,1664]{2,1,0:T(8,128)(2,1)} %constant.2.clone.tables), custom_call_target="tpu_custom_call" | custom-call | tf_op jit(solution)/shard_map/pallas_call | solution.py:499
  134.8 3.3 %shard_map.104 = (bf16[128,1664]{1,0:T(8,128)(2,1)}, bf16[128,1664]{1,0:T(8,128)(2,1)}, bf16[832,512]{1,0:T(8,128)(2,1)}) custom-call(bf16[128,1664]{1,0:T(8,128)(2,1)} %get-tuple-element.6.gg_in, bf16[128,1664]{1,0:T(8,128)(2,1)} %get-tuple-element.7.gu_in, bf16[832,512]{1,0:T(8,128)(2,1)} %get-tuple-element.8.summed, bf16[832,512]{1,0:T(8,128)(2,1)} %latent.1, ...), custom_call_target="tpu_custom_call" | custom-call | tf_op jit(solution)/shard_map/pallas_call | solution.py:534

commit v11 on v8

--- a/solution.py
+++ b/solution.py
@@ -33,12 +33,12 @@
     return pl.multiple_of(value, multiple)
 
 
-CHUNKS = ((0, 768), (768, 512), (1280, 384))
-ROWS = ((0, 384), (384, 640), (640, 832))
+CHUNKS = ((0, 768), (768, 768), (1536, 128))
+ROWS = ((0, 384), (384, 768), (768, 832))
 PIECES = (
     ((0, 0, 0, 384, 0), (1, 1, 384, 384, 0)),
-    ((2, 0, 768, 256, 384), (3, 1, 1024, 256, 384)),
-    ((4, 0, 1280, 256, 640), (5, 1, 1408, 256, 640)),
+    ((2, 0, 768, 384, 384), (3, 1, 1152, 384, 384)),
+    ((4, 0, 1536, 128, 768), (5, 1, 1536, 128, 768)),
 )
 
 
@@ -422,14 +422,8 @@
             def flip(t):
                 return landed[:, at + 128 * t : at + 128 * (t + 1)].astype(F32).T.astype(BF)
 
-            if width == 256 and at == 640:
-                one, two = flip(0), flip(1)
-                if core == 0:
-                    gw_out[640:768, :] = one
-                    gw_out[768:832, :] = two[:64]
-                else:
-                    gw_out[640:704, :] = one[64:]
-                    gw_out[704:832, :] = two
+            if at == 768:
+                gw_out[768:832, :] = flip(0)[64 * core : 64 * core + 64]
             else:
                 for t in range(width // 128):
                     gw_out[at + 128 * t : at + 128 * (t + 1), :] = flip(t)

time: 135 us -> 135 us (level)
  no operation moved by 1% of the time
where the time goes in v11:
time: 135 us; the launch traced here: 134 us
  Pallas kernels  134 us (99%)
    pallas_call x1, Pallas kernels, local(): pl.pallas_call(kernel, out_shape=(jax.ShapeDtypeStruct((TOK, UN), BF), ja...  131 us
    pallas_call x1, Pallas kernels, local(): pl.pallas_call(last, out_shape=(jax.ShapeDtypeStruct((TOK, UN), BF), jax....  3.25 us

profile of v11, /device:TPU:1, one launch (start us, length us, event | category | flops | bytes accessed | tf_op | source)
XLA Modules:
  0.0 134.5 jit_solution(15055723837804736169)
XLA Ops:
  0.6 130.6 %shard_map.103 = (bf16[128,1664]{1,0:T(8,128)(2,1)}, bf16[128,1664]{1,0:T(8,128)(2,1)}, bf16[832,512]{1,0:T(8,128)(2,1)}) custom-call(bf16[128,1664]{1,0:T(8,128)(2,1)} %gate.1, bf16[128,1664]{1,0:T(8,128)(2,1)} %up.1, bf16[128,1664]{1,0:T(8,128)(2,1)} %grot.1, bf16[128,512]{1,0:T(8,128)(2,1)} %gout.1, bf16[2,1664,1664]{2,1,0:T(8,128)(2,1)} %constant.2.clone.tables), custom_call_target="tpu_custom_call" | custom-call | tf_op jit(solution)/shard_map/pallas_call | solution.py:490
  131.2 3.3 %shard_map.104 = (bf16[128,1664]{1,0:T(8,128)(2,1)}, bf16[128,1664]{1,0:T(8,128)(2,1)}, bf16[832,512]{1,0:T(8,128)(2,1)}) custom-call(bf16[128,1664]{1,0:T(8,128)(2,1)} %get-tuple-element.6.gg_in, bf16[128,1664]{1,0:T(8,128)(2,1)} %get-tuple-element.7.gu_in, bf16[832,512]{1,0:T(8,128)(2,1)} %get-tuple-element.8.summed, bf16[832,512]{1,0:T(8,128)(2,1)} %latent.1, ...), custom_call_target="tpu_custom_call" | custom-call | tf_op jit(solution)/shard_map/pallas_call | solution.py:525
